TPU v7x, 32 devices: a whole 2x2x4 slice. The times are simulated.
32 devices in a mesh: group: 4 (over y, x), member: 8 (over z, core).
Axes of the slice: x: 2, y: 2, z: 4, core: 2. Of those that a mesh axis runs over, the one named last changes fastest.
Arguments:
- a_band: bfloat16 [6144, 3, 64, 64], P(('group', 'member')), as said below
- p_tent: bfloat16 [6144, 6, 64], P(('group', 'member')), may hold values from -0.8984375 to 0.8984375
- new_owner: int32 [6144], P(('group', 'member')), may hold values from 0 to 7, as said below
Outputs:
- p_smooth: bfloat16 [6144, 3, 6, 64], P(('group', 'member'))
- coarse: float32 [6144, 252], P(('group', 'member'))
Inputs may be any that keep to these rules, and one draw needn't show every extreme that they name: `new_owner`: within each group, every device sends between 1 and 48 of its block rows to every member of its group, exactly 48 to at least one member, and every member receives exactly 192 block rows. a_band[n, 1, i, i] lies between 2 and 6.
All inputs are finite; a program needn't handle non-finite values.
Results may differ from a plain program's by a relative error of at most 0.0027.
The roundings to bfloat16 on the way count: a program that leaves them out, or rounds other values in their place, can miss the bound.
Values may be sent and summed in bfloat16 or wider, within the bound.
A program may use at most 128 MiB of HBM per device.

v0:
```python
import jax
import jax.numpy as jnp
from jax import lax
from jax.sharding import PartitionSpec as P


def extended(cells, sides, width):
    for axis, dim in sides:
        count = lax.axis_size(axis)
        ends = count - 1
        head = lax.slice_in_dim(cells, 0, width, axis=dim)
        tail = lax.slice_in_dim(cells, cells.shape[dim] - width, cells.shape[dim], axis=dim)
        cells = jnp.concatenate(
            [
                lax.ppermute(tail, axis, [(i, (i + 1) % count) for i in range(ends)]),
                cells,
                lax.ppermute(head, axis, [((i + 1) % count, i) for i in range(ends)]),
            ],
            axis=dim,
        )
    return cells


def slot_sources(flat_slot, rows, members, slots):
    spots = jnp.arange(members * slots, dtype=jnp.int32)
    match = (flat_slot[:, None] == spots[None, :]).astype(jnp.int32)
    return jnp.sum(jnp.arange(rows, dtype=jnp.int32)[:, None] * match, 0)


def to_slots(values, source, members, slots):
    return values[source].reshape((members, slots) + values.shape[1:])


def from_slots(received, take):
    flat = received.reshape((-1,) + received.shape[2:])
    return flat[take]


def placing(got, rows, slots):
    starts = jnp.cumsum(got) - got
    within = jnp.arange(slots, dtype=jnp.int32)
    spots = starts[:, None] + within[None, :]
    landing = jnp.where(within[None, :] < got[:, None], spots, rows).reshape(-1)
    match = (landing[None, :] == jnp.arange(rows, dtype=jnp.int32)[:, None]).astype(jnp.int32)
    take = jnp.sum(jnp.arange(landing.shape[0], dtype=jnp.int32)[None, :] * match, 1)
    pick = jnp.minimum(spots, rows - 1).reshape(-1)
    return (take, pick)


def rim_of_tent(p_rows):
    return extended(p_rows, ((("group", "member"), 0),), 1)


def rim_of_smooth(s_rows):
    return extended(s_rows, ((("group", "member"), 0),), 1)


def smooth_rows(a_rows, earlier, own, later):
    dinv = 1.0 / jnp.diagonal(a_rows[:, 1], axis1=1, axis2=2).astype(jnp.float32)
    own_wide = own.astype(jnp.float32)
    tiles = []
    for k, other in enumerate((earlier, own, later)):
        prod = jnp.einsum("nij,ncj->nci", a_rows[:, k], other, preferred_element_type=jnp.float32)
        base = own_wide if k == 1 else jnp.zeros_like(own_wide)
        tiles.append(base - 0.6 * dinv[:, None, :] * prod)
    return jnp.stack(tiles, 1).astype(jnp.bfloat16)


def product_rows(a_rows, earlier, own, later):
    total = jnp.zeros((own.shape[0], 5) + own.shape[2:], jnp.float32)
    for k, other in enumerate((earlier, own, later)):
        prod = jnp.einsum("nij,ntcj->ntci", a_rows[:, k], other, preferred_element_type=jnp.float32)
        total = total + jnp.pad(prod, ((0, 0), (k, 2 - k), (0, 0), (0, 0)))
    return total.astype(jnp.bfloat16)


def per_device(a_band, p_tent, new_owner):
    members = lax.axis_size("member")
    rows = a_band.shape[0]
    slots = 2 * rows // members
    modes = p_tent.shape[1]
    onehot = (new_owner[:, None] == jnp.arange(members, dtype=jnp.int32)[None, :]).astype(jnp.int32)
    before = jnp.cumsum(onehot, 0) - onehot
    place = jnp.sum(before * onehot, 1)
    counts = jnp.sum(onehot, 0)
    flat_slot = new_owner * slots + place
    source = slot_sources(flat_slot, rows, members, slots)
    a_recv, p_recv, got = (
        lax.all_to_all(
            to_slots(a_band, source, members, slots),
            "member",
            split_axis=0,
            concat_axis=0,
            tiled=True,
        ),
        lax.all_to_all(
            to_slots(p_tent, source, members, slots),
            "member",
            split_axis=0,
            concat_axis=0,
            tiled=True,
        ),
        lax.all_to_all(counts, "member", split_axis=0, concat_axis=0, tiled=True),
    )
    take, pick = placing(got, rows, slots)
    a_new = from_slots(a_recv, take)
    p_new = from_slots(p_recv, take)
    p_rim = rim_of_tent(p_new)
    p_smooth = smooth_rows(a_new, p_rim[:-2], p_new, p_rim[2:])
    s_rim = rim_of_smooth(p_smooth)
    ap_tiles = product_rows(a_new, s_rim[:-2], p_smooth, s_rim[2:])
    stacked = jnp.concatenate([p_smooth, ap_tiles], 1)
    b_rim = extended(stacked, ((("group", "member"), 0),), 1)
    coarse = jnp.zeros((rows, 7, modes, modes), jnp.float32)
    for shift_n in (-1, 0, 1):
        near = b_rim[1 + shift_n : 1 + shift_n + rows]
        term = jnp.einsum(
            "nci,nedi->necd", near[:, 1 - shift_n], near[:, 3:8], preferred_element_type=jnp.float32
        )
        coarse = coarse + jnp.pad(term, ((0, 0), (1 + shift_n, 1 - shift_n), (0, 0), (0, 0)))
    return (p_smooth, coarse.reshape(rows, 7 * modes * modes))


def solution(mesh):
    in_specs = (
        P(("group", "member"), None, None, None),
        P(("group", "member"), None, None),
        P(("group", "member")),
    )
    out_specs = (P(("group", "member"), None, None, None), P(("group", "member"), None))
    return jax.shard_map(
        per_device, mesh=mesh, in_specs=in_specs, out_specs=out_specs, check_vma=False
    )
```

profile of v0, /device:TPU:27, one launch (start us, length us, event | category | flops | bytes accessed | tf_op | source)
XLA Modules:
  0.0 380.8 jit_solution(16587648634318901436)
XLA Ops:
  0.6 0.7 iota_compare_fusion.2
  1.3 0.6 reduce-window.18
  1.9 0.2 slice_reduce_fusion
  2.2 0.1 add_bitcast_fusion
  2.2 0.8 convert_reduce_fusion
  3.1 0.7 copy.124
  3.7 5.4 %all-to-all-start.1 = ((s32[8,1,1]{2,1,0:T(1,128)}), s32[8,1,1]{2,1,0:T(1,128)S(1)}, u32[]{:S(2)}, u32[]{:S(2)}) async-start(s32[8,1,1]{2,1,0:T(1,128)} %copy.124), calls=%async_computation.1 | async-start | bytes 8192 | tf_op jit(solution)/shard_map/all_to_all | solution.py:103
  9.1 0.7 multiply_add_fusion
  9.8 0.1 select_reduce_fusion.1
  10.0 1.2 copy.129
  11.2 1.7 gather_fusion.3
  12.9 0.1 copy.167
  13.0 1.1 reshape.189
  14.1 0.0 all-to-all-done.1
  14.1 5.1 %all-to-all-start.2 = ((bf16[8,2,9216]{2,1,0:T(2,128)(2,1)}), bf16[8,2,9216]{2,1,0:T(2,128)(2,1)S(1)}, u32[]{:S(2)}, u32[]{:S(2)}) async-start(bf16[8,2,9216]{2,1,0:T(2,128)(2,1)} %reshape.189), calls=%async_computation.2 | async-start | bytes 589824 | tf_op jit(solution)/shard_map/all_to_all | solution.py:96
  19.2 13.1 %copy.120 = bf16[192,3,64,64]{3,2,1,0:T(8,128)(2,1)} copy(bf16[192,3,64,64]{0,3,2,1:T(8,128)(2,1)} %param.3) | data formatting | bytes 9437184 | tf_op args[0]
  32.3 17.2 %gather_fusion = bf16[384,3,64,64]{3,2,1,0:T(8,128)(2,1)} fusion(bf16[192,3,64,64]{3,2,1,0:T(8,128)(2,1)} %copy.120, s32[1024]{0:T(1024)S(1)} %pad_clamp_fusion.1), kind=kCustom, calls=%fused_computation | custom fusion | bytes 18875904 | tf_op jit(solution)/shard_map/gather | solution.py:31
  49.5 18.4 %reshape.187 = bf16[8,2,294912]{2,1,0:T(2,128)(2,1)} reshape(bf16[8,48,3,64,64]{4,3,2,1,0:T(8,128)(2,1)} %bitcast.129) | data formatting | bytes 18874368
  67.8 5.1 %all-to-all-start = ((bf16[8,2,294912]{2,1,0:T(2,128)(2,1)}), bf16[8,2,294912]{2,1,0:T(2,128)(2,1)}, u32[]{:S(2)}, u32[]{:S(2)}) async-start(bf16[8,2,294912]{2,1,0:T(2,128)(2,1)} %reshape.187), calls=%async_computation | async-start | bytes 18874368 | tf_op jit(solution)/shard_map/all_to_all | solution.py:89
  73.0 0.2 reduce.2
  73.2 0.2 reduce-window.20
  73.4 0.1 add_select_fusion
  73.5 0.1 select_n.39
  73.5 0.1 select_reduce_fusion
  73.7 0.4 reshape.190
  74.1 0.2 copy.155
  74.3 0.7 gather_fusion.4
  75.1 2.3 collective-permute-start.1
  77.3 7.1 %collective-permute-start = (bf16[1,6,64]{2,1,0:T(8,128)(2,1)S(1)}, bf16[1,6,64]{2,1,0:T(8,128)(2,1)S(1)}, u32[]{:S(2)}, u32[]{:S(2)}) collective-permute-start(bf16[1,6,64]{2,1,0:T(8,128)(2,1)S(1)} %get-tuple-element.20), channel_id=1, source_target_pairs={{0,1},{1,2},{2,3},{3,4},{4,5},{5,6},{6,7},{7,8},{8,9},{9,10},{10,1... | collective-permute-start | bytes 2312 | tf_op jit(solution)/shard_map/ppermute | solution.py:15
  84.4 142.4 %collective-permute-done.1 = bf16[1,6,64]{2,1,0:T(8,128)(2,1)S(1)} collective-permute-done((bf16[1,6,64]{2,1,0:T(8,128)(2,1)S(1)}, bf16[1,6,64]{2,1,0:T(8,128)(2,1)S(1)}, u32[]{:S(2)}, u32[]{:S(2)}) %collective-permute-start.1) | collective-permute-done | bytes 800 | tf_op jit(solution)/shard_map/ppermute | solution.py:17
  226.9 0.9 fusion.122
  227.7 0.9 fusion.120
  228.6 48.2 %all-to-all-done = bf16[8,2,294912]{2,1,0:T(2,128)(2,1)} async-done(((bf16[8,2,294912]{2,1,0:T(2,128)(2,1)}), bf16[8,2,294912]{2,1,0:T(2,128)(2,1)}, u32[]{:S(2)}, u32[]{:S(2)}) %all-to-all-start) | async-done | bytes 9437216 | tf_op jit(solution)/shard_map/all_to_all | solution.py:89
  276.8 18.0 %reshape.188 = bf16[8,48,3,64,64]{4,3,2,1,0:T(8,128)(2,1)} reshape(bf16[8,2,294912]{2,1,0:T(2,128)(2,1)} %all-to-all-done) | data formatting | bytes 18874368
  294.8 16.1 %gather_fusion.1 = bf16[192,3,64,64]{3,2,1,0:T(8,128)(2,1)} fusion(bf16[384,3,64,64]{3,2,1,0:T(8,128)(2,1)} %bitcast.132, s32[1024]{0:T(1024)S(1)} %pad_clamp_fusion), kind=kCustom, calls=%fused_computation.1 | custom fusion | bytes 9437952 | tf_op jit(solution)/shard_map/gather | solution.py:36
  311.0 2.6 slice_bitcast_fusion
  313.6 3.8 copy.127
  317.4 1.6 gather_fusion.2
  319.0 0.1 copy.128
  319.1 3.8 fusion.56
  322.9 0.0 slice-start.2
  322.9 3.8 fusion.60
  326.7 0.0 slice-done.2
  326.8 1.7 fusion.57
  328.5 0.4 pad_maximum_fusion.6
  328.9 2.4 collective-permute-start.3
  331.3 7.0 %collective-permute-start.2 = (bf16[1,3,6,64]{3,2,0,1:T(8,128)(2,1)S(1)}, bf16[1,3,6,64]{3,2,0,1:T(8,128)(2,1)S(1)}, u32[]{:S(2)}, u32[]{:S(2)}) collective-permute-start(bf16[1,3,6,64]{3,2,0,1:T(8,128)(2,1)S(1)} %get-tuple-element.19), channel_id=1, source_target_pairs={{0,1},{1,2},{2,3},{3,4},{4,5},{5,6},{6,7},{7,8},{8,9},{9,10},{10,1... | collective-permute-start | bytes 6920 | tf_op jit(solution)/shard_map/ppermute | solution.py:15
  338.3 3.6 fusion.22
  341.9 1.8 copy.143
  343.7 0.4 pad_maximum_fusion
  344.2 3.8 fusion.24
  348.0 3.8 add_convert_fusion
  351.8 0.6 pad_maximum_fusion.10
  352.4 1.9 collective-permute-start.5
  354.3 2.7 convolution_bitcast_fusion
  357.1 7.2 %collective-permute-start.4 = (bf16[1,8,6,64]{3,2,1,0:T(8,128)(2,1)}, bf16[1,8,6,64]{3,2,1,0:T(8,128)(2,1)}, u32[]{:S(2)}, u32[]{:S(2)}) collective-permute-start(bf16[1,8,6,64]{3,2,1,0:T(8,128)(2,1)} %get-tuple-element.14), channel_id=1, source_target_pairs={{0,1},{1,2},{2,3},{3,4},{4,5},{5,6},{6,7},{7,8},{8,9},{9,10},{10,1... | collective-permute-start | bytes 18440 | tf_op jit(solution)/shard_map/ppermute | solution.py:15
  364.3 0.2 maximum_bitcast_fusion.10
  364.5 3.3 fusion.35
  367.7 0.8 maximum_bitcast_fusion.11
  368.6 2.2 fusion.38
  370.8 1.1 copy-done.2
  371.9 3.3 pad_add_fusion
  375.2 4.8 %copy.142 = f32[192,7,6,6]{0,3,2,1:T(8,128)S(1)} copy(f32[192,7,6,6]{2,3,1,0:T(8,128)} %pad_add_fusion) | data formatting | bytes 387072 | tf_op jit(solution)/shard_map/add | solution.py:120
  380.0 0.8 copy.144
  (33 shorter events, 0.2 us)
Async XLA Ops:
  3.7 10.3 %all-to-all-start.1 = ((s32[8,1,1]{2,1,0:T(1,128)}), s32[8,1,1]{2,1,0:T(1,128)S(1)}, u32[]{:S(2)}, u32[]{:S(2)}) async-start(s32[8,1,1]{2,1,0:T(1,128)} %copy.124), calls=%async_computation.1 | async-start | bytes 8192 | tf_op jit(solution)/shard_map/all_to_all | solution.py:103
  14.1 53.8 %all-to-all-start.2 = ((bf16[8,2,9216]{2,1,0:T(2,128)(2,1)}), bf16[8,2,9216]{2,1,0:T(2,128)(2,1)S(1)}, u32[]{:S(2)}, u32[]{:S(2)}) async-start(bf16[8,2,9216]{2,1,0:T(2,128)(2,1)} %reshape.189), calls=%async_computation.2 | async-start | bytes 589824 | tf_op jit(solution)/shard_map/all_to_all | solution.py:96
  67.8 209.0 %all-to-all-start = ((bf16[8,2,294912]{2,1,0:T(2,128)(2,1)}), bf16[8,2,294912]{2,1,0:T(2,128)(2,1)}, u32[]{:S(2)}, u32[]{:S(2)}) async-start(bf16[8,2,294912]{2,1,0:T(2,128)(2,1)} %reshape.187), calls=%async_computation | async-start | bytes 18874368 | tf_op jit(solution)/shard_map/all_to_all | solution.py:89
  75.1 151.8 %collective-permute-start.1 = (bf16[1,6,64]{2,1,0:T(8,128)(2,1)S(1)}, bf16[1,6,64]{2,1,0:T(8,128)(2,1)S(1)}, u32[]{:S(2)}, u32[]{:S(2)}) collective-permute-start(bf16[1,6,64]{2,1,0:T(8,128)(2,1)S(1)} %get-tuple-element.21), channel_id=1, source_target_pairs={{1,0},{2,1},{3,2},{4,3},{5,4},{6,5},{7,6},{8,7},{9,8},{10,9},{11,1... | collective-permute-start | bytes 2312 | tf_op jit(solution)/shard_map/ppermute | solution.py:17
  77.3 150.4 %collective-permute-start = (bf16[1,6,64]{2,1,0:T(8,128)(2,1)S(1)}, bf16[1,6,64]{2,1,0:T(8,128)(2,1)S(1)}, u32[]{:S(2)}, u32[]{:S(2)}) collective-permute-start(bf16[1,6,64]{2,1,0:T(8,128)(2,1)S(1)} %get-tuple-element.20), channel_id=1, source_target_pairs={{0,1},{1,2},{2,3},{3,4},{4,5},{5,6},{6,7},{7,8},{8,9},{9,10},{10,1... | collective-permute-start | bytes 2312 | tf_op jit(solution)/shard_map/ppermute | solution.py:15
  317.4 5.5 %copy-start.3 = (bf16[193,6,64]{2,1,0:T(8,128)(2,1)S(1)}, bf16[193,6,64]{2,1,0:T(8,128)(2,1)}, u32[]{:S(2)}) copy-start(bf16[193,6,64]{2,1,0:T(8,128)(2,1)} %fusion.122) | copy-start | bytes 444676
  319.1 7.6 %slice-start = ((s8[9437184]{0:T(1024)(128)(4,1)}), s8[4194304]{0:T(1024)(128)(4,1)S(1)}, s32[]{:S(2)}) async-start(s8[9437184]{0:T(1024)(128)(4,1)} %bitcast.130), calls=%async_computation.3 | async-start | bytes 8388608
  322.9 3.8 %slice-start.1 = ((s8[9437184]{0:T(1024)(128)(4,1)}), s8[4194304]{0:T(1024)(128)(4,1)S(1)}, s32[]{:S(2)}) async-start(s8[9437184]{0:T(1024)(128)(4,1)} %bitcast.130), calls=%async_computation.4 | async-start | bytes 8388608
  322.9 3.8 %slice-start.2 = ((s8[9437184]{0:T(1024)(128)(4,1)}), s8[1048576]{0:T(1024)(128)(4,1)S(1)}, s32[]{:S(2)}) async-start(s8[9437184]{0:T(1024)(128)(4,1)} %bitcast.130), calls=%async_computation.5 | async-start | bytes 2097152
  322.9 3.8 %copy-start.4 = (bf16[193,6,64]{2,1,0:T(8,128)(2,1)S(1)}, bf16[193,6,64]{2,1,0:T(8,128)(2,1)}, u32[]{:S(2)}) copy-start(bf16[193,6,64]{2,1,0:T(8,128)(2,1)} %fusion.120) | copy-start | bytes 444676
  328.9 14.8 %collective-permute-start.3 = (bf16[1,3,6,64]{3,2,0,1:T(8,128)(2,1)S(1)}, bf16[1,3,6,64]{3,2,0,1:T(8,128)(2,1)S(1)}, u32[]{:S(2)}, u32[]{:S(2)}) collective-permute-start(bf16[1,3,6,64]{3,2,0,1:T(8,128)(2,1)S(1)} %get-tuple-element.18), channel_id=1, source_target_pairs={{1,0},{2,1},{3,2},{4,3},{5,4},{6,5},{7,6},{8,7},{9,8},{10,9},{11,1... | collective-permute-start | bytes 6920 | tf_op jit(solution)/shard_map/ppermute | solution.py:17
  331.3 12.4 %collective-permute-start.2 = (bf16[1,3,6,64]{3,2,0,1:T(8,128)(2,1)S(1)}, bf16[1,3,6,64]{3,2,0,1:T(8,128)(2,1)S(1)}, u32[]{:S(2)}, u32[]{:S(2)}) collective-permute-start(bf16[1,3,6,64]{3,2,0,1:T(8,128)(2,1)S(1)} %get-tuple-element.19), channel_id=1, source_target_pairs={{0,1},{1,2},{2,3},{3,4},{4,5},{5,6},{6,7},{7,8},{8,9},{9,10},{10,1... | collective-permute-start | bytes 6920 | tf_op jit(solution)/shard_map/ppermute | solution.py:15
  344.2 3.8 %copy-start.1 = (f32[192,5,6,64]{3,2,1,0:T(8,128)S(1)}, f32[192,5,6,64]{3,2,1,0:T(8,128)}, u32[]{:S(2)}) copy-start(f32[192,5,6,64]{3,2,1,0:T(8,128)} %fusion.22) | copy-start | bytes 4423684
  352.4 11.9 %collective-permute-start.5 = (bf16[1,8,6,64]{3,2,1,0:T(8,128)(2,1)S(1)}, bf16[1,8,6,64]{3,2,1,0:T(8,128)(2,1)S(1)}, u32[]{:S(2)}, u32[]{:S(2)}) collective-permute-start(bf16[1,8,6,64]{3,2,1,0:T(8,128)(2,1)S(1)} %get-tuple-element.15), channel_id=1, source_target_pairs={{1,0},{2,1},{3,2},{4,3},{5,4},{6,5},{7,6},{8,7},{9,8},{10,9},{11,1... | collective-permute-start | bytes 18440 | tf_op jit(solution)/shard_map/ppermute | solution.py:17
  357.1 10.7 %collective-permute-start.4 = (bf16[1,8,6,64]{3,2,1,0:T(8,128)(2,1)}, bf16[1,8,6,64]{3,2,1,0:T(8,128)(2,1)}, u32[]{:S(2)}, u32[]{:S(2)}) collective-permute-start(bf16[1,8,6,64]{3,2,1,0:T(8,128)(2,1)} %get-tuple-element.14), channel_id=1, source_target_pairs={{0,1},{1,2},{2,3},{3,4},{4,5},{5,6},{6,7},{7,8},{8,9},{9,10},{10,1... | collective-permute-start | bytes 18440 | tf_op jit(solution)/shard_map/ppermute | solution.py:15
  368.5 2.2 copy-start
  368.6 3.3 copy-start.2
where the time goes:
time: 385 us; the launch traced here: 381 us
  waiting for transfers between devices  191 us (50%)
  local copies, waits for them, and re-layouts  106 us (28%)
  starting transfers between devices  43.5 us (11%)
  matrix products  28.8 us (7%)
  other arithmetic  11.1 us (3%)
    ppermute x3, waiting for transfers between devices, extended(): lax.ppermute(head, axis, [((i + 1) % count, i) for i in range(ends)])  142 us
    unnamed x24, local copies, waits for them, and re-layouts  55.8 us
    all_to_all x1, waiting for transfers between devices, per_device(): lax.all_to_all(to_slots(a_band, source, members, slots), 'member', split_...  48.2 us
    ppermute x3, starting transfers between devices, extended(): lax.ppermute(tail, axis, [(i, (i + 1) % count) for i in range(ends)])  21.3 us
    gather x2, local copies, waits for them, and re-layouts, to_slots(): return values[source].reshape((members, slots) + values.shape[1:])  18.9 us
    gather x2, local copies, waits for them, and re-layouts, from_slots(): return flat[take]  16.9 us
    dot_general x3, matrix products, smooth_rows(): jnp.einsum('nij,ncj->nci', a_rows[:, k], other, preferred_element_type=jn...  9.34 us
    dot_general x3, matrix products, per_device(): jnp.einsum('nci,nedi->necd', near[:, 1 - shift_n], near[:, 3:8], preferre...  8.21 us
  transfers between devices with their start and end apart: 9, of which 2 were waited for; matrix products, arithmetic and copies ran while one was open for 18% of the time, Pallas kernels for 0%

commit v1 on v0

v1 whole, which is shorter than its diff:
```python
import functools

import jax
import jax.numpy as jnp
from jax import lax
from jax.experimental import pallas as pl
from jax.experimental.pallas import tpu as pltpu
from jax.sharding import PartitionSpec as P

HALO = 3
LANES = 128
MESH = pl.DeviceIdType.MESH


def exchange_kernel(members, slots, send_ref, recv_ref, send_sem, recv_sem, own_sem):
    me = lax.axis_index("member")
    barrier = pltpu.get_barrier_semaphore()

    def greet(o, carry):
        pl.semaphore_signal(
            barrier, inc=1, device_id={"member": lax.rem(me + o, members)}, device_id_type=MESH
        )
        return carry

    lax.fori_loop(1, members, greet, 0)
    pl.semaphore_wait(barrier, members - 1)

    def copy(o):
        other = lax.rem(me + o, members)
        return pltpu.make_async_remote_copy(
            src_ref=send_ref.at[pl.ds(pl.multiple_of(other * slots, slots), slots)],
            dst_ref=recv_ref.at[pl.ds(pl.multiple_of(me * slots, slots), slots)],
            send_sem=send_sem.at[o],
            recv_sem=recv_sem.at[o],
            device_id={"member": other},
            device_id_type=MESH,
        )

    def start(o, carry):
        copy(o).start()
        return carry

    def finish(o, carry):
        copy(o).wait()
        return carry

    lax.fori_loop(1, members, start, 0)
    mine = pl.ds(pl.multiple_of(me * slots, slots), slots)
    own = pltpu.make_async_copy(send_ref.at[mine], recv_ref.at[mine], own_sem)
    own.start()
    own.wait()
    lax.fori_loop(1, members, finish, 0)


def exchange(send, members, slots):
    width = send.shape[1]
    return pl.pallas_call(
        functools.partial(exchange_kernel, members, slots),
        out_shape=jax.ShapeDtypeStruct((members * slots + 16, width), send.dtype),
        in_specs=[pl.BlockSpec(memory_space=pl.ANY)],
        out_specs=pl.BlockSpec(memory_space=pl.ANY),
        scratch_shapes=[
            pltpu.SemaphoreType.DMA((members,)),
            pltpu.SemaphoreType.DMA((members,)),
            pltpu.SemaphoreType.DMA,
        ],
        compiler_params=pltpu.CompilerParams(collective_id=0, has_side_effects=True),
        name="exchange_rows",
    )(send)


def shifted(x, k):
    width = x.shape[-1]
    if k == 0:
        return pltpu.roll(x, 1, axis=x.ndim - 1)
    if k == 2:
        return pltpu.roll(x, width - 1, axis=x.ndim - 1)
    return x


def setup_kernel(a_ref, p_ref, dg_ref, s_ref, co_ref, p3, s3, ap3, dinv):
    modes, tile, width = p_ref.shape
    f32 = jnp.float32
    half = tile // 2
    parts = [(i, l) for l in range(width // LANES) for i in range(2)]
    diag = dg_ref[...]
    dinv[...] = jnp.where(diag > 1.0, 1.0 / jnp.where(diag > 1.0, diag, 1.0), 0.0)
    for c in range(modes):
        own = p_ref[c].astype(f32)
        for k in range(3):
            p3[k, c] = shifted(own, k)

    def product(ks, rows, i0, l0):
        lanes = pl.ds(l0, LANES)

        def body(j8, accs):
            accs = list(accs)
            j0 = pl.multiple_of(j8 * 8, 8)
            for k in ks:
                vecs = [ref[pl.ds(j0, 8), lanes] for ref in rows(k)]
                for jj in range(8):
                    a = a_ref[k, j0 + jj, pl.ds(i0, half), lanes].astype(f32)
                    for c in range(modes):
                        accs[c] = accs[c] + a * vecs[c][jj : jj + 1]
            return tuple(accs)

        zero = jnp.zeros((half, LANES), f32)
        return lax.fori_loop(0, tile // 8, body, (zero,) * modes)

    def each_part(fn):
        def body(q, carry):
            fn(
                pl.multiple_of((q % 2) * half, half),
                pl.multiple_of((q // 2) * LANES, LANES),
            )
            return carry

        lax.fori_loop(0, len(parts), body, 0)

    for k in range(3):

        def smooth(i0, l0, k=k):
            accs = product([k], lambda k: [p3.at[k, c] for c in range(modes)], i0, l0)
            inv = 0.6 * dinv[pl.ds(i0, half), pl.ds(l0, LANES)]
            for c in range(modes):
                value = -inv * accs[c]
                if k == 1:
                    value = p3[1, c, pl.ds(i0, half), pl.ds(l0, LANES)] + value
                value = value.astype(jnp.bfloat16)
                s_ref[k, c, pl.ds(i0, half), pl.ds(l0, LANES)] = value
                s3[1, k, c, pl.ds(i0, half), pl.ds(l0, LANES)] = value.astype(f32)

        each_part(smooth)

    def spread_s(q, carry):
        t, c = q // modes, q % modes
        own = s3[1, t, c]
        s3[0, t, c] = shifted(own, 0)
        s3[2, t, c] = shifted(own, 2)
        return carry

    lax.fori_loop(0, 3 * modes, spread_s, 0)

    for e in range(5):

        def prod(i0, l0, e=e):
            ks = [k for k in range(3) if 0 <= e - k <= 2]
            accs = product(ks, lambda k: [s3.at[k, e - k, c] for c in range(modes)], i0, l0)
            for c in range(modes):
                ap3[1, e, c, pl.ds(i0, half), pl.ds(l0, LANES)] = (
                    accs[c].astype(jnp.bfloat16).astype(f32)
                )

        each_part(prod)

    def spread_ap(q, carry):
        e, c = q // modes, q % modes
        own = ap3[1, e, c]
        ap3[0, e, c] = shifted(own, 0)
        ap3[2, e, c] = shifted(own, 2)
        return carry

    lax.fori_loop(0, 5 * modes, spread_ap, 0)

    for f in range(7):

        def coarse(q, carry, f=f):
            c, l0 = q // (width // LANES), pl.multiple_of((q % (width // LANES)) * LANES, LANES)
            lanes = pl.ds(l0, LANES)
            sums = [None] * modes
            for dn in (-1, 0, 1):
                e = f - 1 - dn
                if not 0 <= e <= 4:
                    continue
                s = s3[dn + 1, 1 - dn, c, :, lanes]
                for d in range(modes):
                    term = s * ap3[dn + 1, e, d, :, lanes]
                    term = jnp.sum(term.reshape(tile // 8, 8, LANES), axis=0)
                    sums[d] = term if sums[d] is None else sums[d] + term
            for d in range(modes):
                co_ref[f, c, d : d + 1, lanes] = jnp.sum(sums[d], axis=0, keepdims=True)
            return carry

        lax.fori_loop(0, modes * (width // LANES), coarse, 0)


def setup(a, p, diag):
    modes, tile, width = p.shape
    f32 = jnp.float32
    return pl.pallas_call(
        setup_kernel,
        out_shape=(
            jax.ShapeDtypeStruct((3, modes, tile, width), jnp.bfloat16),
            jax.ShapeDtypeStruct((7, modes, modes, width), f32),
        ),
        in_specs=[pl.BlockSpec(memory_space=pltpu.VMEM)] * 3,
        out_specs=(pl.BlockSpec(memory_space=pltpu.VMEM),) * 2,
        scratch_shapes=[
            pltpu.VMEM((3, modes, tile, width), f32),
            pltpu.VMEM((3, 3, modes, tile, width), f32),
            pltpu.VMEM((3, 5, modes, tile, width), f32),
            pltpu.VMEM((tile, width), f32),
        ],
        compiler_params=pltpu.CompilerParams(vmem_limit_bytes=56 * 1024 * 1024),
        name="coarse_setup",
    )(a, p, diag)


def per_device(a_band, p_tent, new_owner):
    members = lax.axis_size("member")
    me = lax.axis_index("member")
    rows, _, tile, _ = a_band.shape
    modes = p_tent.shape[1]
    cap = 2 * rows // members
    slots = -(-cap // 16) * 16
    bf16, i32 = jnp.bfloat16, jnp.int32
    size = 3 * tile * tile
    width = -(-(rows + 2 * HALO) // LANES) * LANES

    onehot = (new_owner[None, :] == jnp.arange(members, dtype=i32)[:, None]).astype(i32)
    earlier = (jnp.arange(rows)[:, None] < jnp.arange(rows)[None, :]).astype(jnp.float32)
    before = jnp.dot(onehot.astype(jnp.float32), earlier).astype(i32)
    place = jnp.sum(before * onehot, 0)
    counts = jnp.sum(onehot, 1)
    got = lax.all_gather(counts, "member")[:, me]

    flat_slot = new_owner * slots + place
    pick = (jnp.arange(members * slots, dtype=i32)[:, None] == flat_slot[None, :]).astype(bf16)
    dense = jnp.concatenate(
        [
            a_band.transpose(1, 3, 2, 0).reshape(size, rows),
            p_tent.transpose(1, 2, 0).reshape(modes * tile, rows),
        ],
        0,
    )
    send = lax.dot_general(
        pick, dense, (((1,), (1,)), ((), ())), preferred_element_type=jnp.float32
    ).astype(bf16)
    recv = exchange(send, members, slots)

    ends = jnp.sum(
        jnp.where(jnp.arange(members)[None, :] <= jnp.arange(members)[:, None], got[None, :], 0), 1
    )
    starts = ends - got
    within = jnp.arange(slots, dtype=i32)
    lands = jnp.where(within[None, :] < got[:, None], starts[:, None] + within[None, :], -width)
    lands = lands.reshape(-1)
    edge = jnp.arange(16, dtype=i32)
    edge_row = jnp.where(edge < HALO, edge, jnp.where(edge < 2 * HALO, rows - 2 * HALO + edge, -1))
    rim_pick = (edge_row[:, None] == lands[None, :]).astype(bf16)
    rim = jnp.dot(
        rim_pick, recv[: members * slots], preferred_element_type=jnp.float32
    ).astype(bf16)
    axes = ("group", "member")
    devices = lax.axis_size("group") * members
    up = [(i, i + 1) for i in range(devices - 1)]
    down = [(i + 1, i) for i in range(devices - 1)]
    from_left = lax.ppermute(rim[HALO : 2 * HALO], axes, up)
    from_right = lax.ppermute(rim[:HALO], axes, down)
    halo = jnp.concatenate(
        [from_left, from_right, jnp.zeros((16 - 2 * HALO, rim.shape[1]), bf16)], 0
    )
    recv = lax.dynamic_update_slice(recv, halo, (members * slots, 0))
    halo_lane = jnp.where(edge < HALO, edge, jnp.where(edge < 2 * HALO, rows + edge, -1))
    lane = jnp.concatenate([lands + HALO, halo_lane])
    place_out = (lane[:, None] == jnp.arange(width, dtype=i32)[None, :]).astype(bf16)
    ext = lax.dot_general(
        recv, place_out, (((0,), (0,)), ((), ())), preferred_element_type=jnp.float32
    ).astype(bf16)
    a = ext[:size].reshape(3, tile, tile, width)
    p = ext[size:].reshape(modes, tile, width)
    eye = jnp.eye(tile, dtype=bf16)[:, :, None]
    diag = jnp.sum((a[1] * eye).astype(jnp.float32), 0)
    s_out, co = setup(a, p, diag)
    p_smooth = s_out[..., HALO : HALO + rows].transpose(3, 0, 1, 2)
    coarse = co[..., HALO : HALO + rows].reshape(7 * modes * modes, rows).T
    return (p_smooth, coarse)


def solution(mesh):
    in_specs = (
        P(("group", "member"), None, None, None),
        P(("group", "member"), None, None),
        P(("group", "member")),
    )
    out_specs = (P(("group", "member"), None, None, None), P(("group", "member"), None))
    return jax.shard_map(
        per_device, mesh=mesh, in_specs=in_specs, out_specs=out_specs, check_vma=False
    )
```

time: 385 us -> 313 us (0.81)
  Pallas kernels: 0 us -> 254 us
  waiting for transfers between devices: 191 us -> 6.83 us
  local copies, waits for them, and re-layouts: 106 us -> 19.1 us
  starting transfers between devices: 43.5 us -> 4.64 us
  matrix products: 28.8 us -> 19.7 us
  other arithmetic: 11.1 us -> 2.75 us
  blocking collectives: 0 us -> 4.24 us
    pallas_call x0 -> x2, Pallas kernels: none -> 254 us  [the longest x1 216 us: exchange(): pl.pallas_call(functools.partial(exchange_kernel, members, slots), out_sh...]
    ppermute x6 -> x2, waiting for transfers between devices: 142 us -> 6.83 us  [the longest x1 6.83 us: per_device(): from_right = lax.ppermute(rim[:HALO], axes, down)]
    unnamed x24 -> x10, local copies, waits for them, and re-layouts: 55.8 us -> 2.3 us
    all_to_all x3 -> x0, waiting for transfers between devices: 48.2 us -> none  [the longest x1 48.2 us: per_device(): lax.all_to_all(to_slots(a_band, source, members, slots), 'member', split_...]
    gather x5 -> x0, local copies, waits for them, and re-layouts: 37.4 us -> none  [the longest x2 18.9 us: to_slots(): return values[source].reshape((members, slots) + values.shape[1:])]
    ppermute x6 -> x2, starting transfers between devices: 27.9 us -> 4.64 us  [the longest x1 2.59 us: per_device(): from_right = lax.ppermute(rim[:HALO], axes, down)]
    all_to_all x3 -> x0, starting transfers between devices: 15.6 us -> none  [the longest x1 5.41 us: per_device(): lax.all_to_all(counts, 'member', split_axis=0, concat_axis=0, tiled=True)]
    transpose x0 -> x2, local copies, waits for them, and re-layouts: none -> 11.2 us  [the longest x1 9.09 us: per_device(): a_band.transpose(1, 3, 2, 0).reshape(size, rows)]
  transfers between devices with their start and end apart: 9 -> 2, of which waited for: 2 -> 1; matrix products, arithmetic and copies ran while one was open for 18% -> 0% of each run, Pallas kernels for 0% -> 0%
where the time goes in v1:
time: 313 us; the launch traced here: 312 us
  Pallas kernels  254 us (81%)
  matrix products  19.7 us (6%)
  local copies, waits for them, and re-layouts  19.1 us (6%)
  waiting for transfers between devices  6.83 us (2%)
  starting transfers between devices  4.64 us (1%)
  blocking collectives  4.24 us (1%)
    pallas_call x1, Pallas kernels, exchange(): pl.pallas_call(functools.partial(exchange_kernel, members, slots), out_sh...  216 us
    pallas_call x1, Pallas kernels, setup(): pl.pallas_call(setup_kernel, out_shape=(jax.ShapeDtypeStruct((3, modes, t...  38.1 us
    dot_general x1, matrix products, per_device(): lax.dot_general(pick, dense, (((1,), (1,)), ((), ())), preferred_element_...  9.28 us
    transpose x1, local copies, waits for them, and re-layouts, per_device(): a_band.transpose(1, 3, 2, 0).reshape(size, rows)  9.09 us
    ppermute x1, waiting for transfers between devices, per_device(): from_right = lax.ppermute(rim[:HALO], axes, down)  6.83 us
  transfers between devices with their start and end apart: 2, of which 1 were waited for; matrix products, arithmetic and copies ran while one was open for 0% of the time, Pallas kernels for 0%

profile of v1, /device:TPU:27, one launch (start us, length us, event | category | flops | bytes accessed | tf_op | source)
XLA Modules:
  0.0 312.5 jit_solution(8096561221246837180)
XLA Ops:
  0.6 0.0 copy-start.1
  0.6 0.0 copy-start.2
  0.7 0.8 convert_reduce_fusion.1
  1.5 0.9 fusion.5
  2.4 1.2 dynamic-slice
  4.3 0.2 dynamic-update-slice
  4.6 0.1 reshape.86
  4.7 4.2 %all-reduce.1 = s32[8,8]{1,0:T(8,128)S(1)} all-reduce(s32[8,8]{1,0:T(8,128)S(1)} %reshape.86), channel_id=2, replica_groups=mesh['group'=4,'member'=8] {'member'}, use_global_device_ids=true, to_apply=%add | all-reduce | flops 64 | bytes 512
  8.9 0.2 dynamic-slice_reduce_fusion
  9.1 0.1 select_reduce_fusion
  9.2 0.1 copy.11
  9.3 0.2 subtract_reduce_fusion
  9.5 0.1 add_select_fusion
  9.5 0.1 select_n.46
  9.6 9.1 %copy.10 = bf16[3,64,64,192]{3,2,1,0:T(8,128)(2,1)} copy(bf16[3,64,64,192]{3,1,2,0:T(8,128)(2,1)} %bitcast.16) | data formatting | bytes 9437184 | tf_op jit(solution)/shard_map/transpose | solution.py:231
  18.7 0.0 copy-done.1
  18.7 0.0 copy-done.2
  18.7 9.3 %convolution_convert_fusion.send_ref = bf16[384,12672]{1,0:T(8,128)(2,1)} fusion(bf16[384,192]{1,0:T(8,128)(2,1)S(1)} %bitcast.21, bf16[12288,192]{1,0:T(8,128)(2,1)} %bitcast.17, s32[192]{0:T(256)S(1)} %multiply_add_fusion), kind=kOutput, calls=%fused_computation | convolution fusion | flops 1883234304 | bytes 14598912 | tf_op jit(solution)/shard_map/dot_general | solution.py:236
  28.0 215.7 %exchange_rows.1 = bf16[400,12672]{1,0:T(8,128)(2,1)} custom-call(bf16[384,12672]{1,0:T(8,128)(2,1)} %convolution_convert_fusion.send_ref), custom_call_target="tpu_custom_call" | custom-call | tf_op jit(solution)/shard_map/exchange_rows/pallas_call | solution.py:57
  243.8 0.0 copy-start
  243.8 5.3 %convolution_convert_fusion.2 = bf16[16,12672]{1,0:T(8,128)(2,1)S(1)} fusion(bf16[400,12672]{1,0:T(8,128)(2,1)} %exchange_rows.1, s32[384]{0:T(512)S(1)} %select_n.46, s32[16]{0:T(128)S(1)} %compare_select_fusion.1), kind=kOutput, calls=%fused_computation.2 | convolution fusion | flops 155922432 | bytes 10139200 | tf_op jit(solution)/shard_map/dot_general | solution.py:251
  249.1 0.1 fusion.16
  249.2 2.1 collective-permute-start
  251.2 2.6 collective-permute-start.1
  253.9 0.1 pad.4.clone
  254.0 0.0 collective-permute-done
  254.0 6.8 %collective-permute-done.1 = bf16[3,12672]{1,0:T(4,128)(2,1)S(1)} collective-permute-done((bf16[3,12672]{1,0:T(4,128)(2,1)S(1)}, bf16[3,12672]{1,0:T(4,128)(2,1)S(1)}, u32[]{:S(2)}, u32[]{:S(2)}) %collective-permute-start.1) | collective-permute-done | bytes 76064 | tf_op jit(solution)/shard_map/ppermute | solution.py:259
  260.8 0.0 copy-done
  260.8 0.2 maximum_dynamic-update-slice_fusion
  261.0 4.2 %convolution_convert_fusion.1 = bf16[12672,256]{1,0:T(8,128)(2,1)S(1)} fusion(bf16[400,12672]{1,0:T(8,128)(2,1)S(1)} %maximum_dynamic-update-slice_fusion, s32[400]{0:T(512)S(1)} %pad_add_fusion), kind=kOutput, calls=%fused_computation.1 | convolution fusion | flops 2598572032 | bytes 16627264 | tf_op jit(solution)/shard_map/dot_general | solution.py:267
  265.2 3.0 slice.36
  268.1 0.1 slice.38
  268.3 0.7 slice.37
  269.0 1.3 convert_reduce_fusion.dg_ref
  270.3 38.1 %coarse_setup.1 = (bf16[3,6,64,256]{3,2,1,0:T(8,128)(2,1)}, f32[7,6,6,256]{3,2,1,0:T(8,128)}) custom-call(bf16[3,64,64,256]{3,2,1,0:T(8,128)(2,1)} %bitcast.14, bf16[6,64,256]{2,1,0:T(8,128)(2,1)} %bitcast.19, f32[64,256]{1,0:T(8,128)} %convert_reduce_fusion.dg_ref), custom_call_target="tpu_custom_call" | custom-call | tf_op jit(solution)/shard_map/coarse_setup/pallas_call | solution.py:190
  308.4 1.1 slice.33
  309.5 0.8 copy.12
  310.3 2.1 slice_bitcast_fusion
  (9 shorter events, 0.1 us)
Async XLA Ops:
  0.6 18.1 %copy-start.1 = (s32[192]{0:T(256)S(1)}, s32[192]{0:T(256)}, u32[]{:S(2)}) copy-start(s32[192]{0:T(256)} %param.5) | copy-start | bytes 2308
  0.6 18.1 %copy-start.2 = (bf16[192,6,64]{0,2,1:T(8,128)(2,1)S(1)}, bf16[192,6,64]{0,2,1:T(8,128)(2,1)}, u32[]{:S(2)}) copy-start(bf16[192,6,64]{0,2,1:T(8,128)(2,1)} %param.4) | copy-start | bytes 442372
  243.8 17.1 %copy-start = (bf16[400,12672]{1,0:T(8,128)(2,1)S(1)}, bf16[400,12672]{1,0:T(8,128)(2,1)}, u32[]{:S(2)}) copy-start(bf16[400,12672]{1,0:T(8,128)(2,1)} %exchange_rows.1) | copy-start | bytes 30412804
  249.2 4.8 %collective-permute-start = (bf16[3,12672]{1,0:T(4,128)(2,1)S(1)}, bf16[3,12672]{1,0:T(4,128)(2,1)S(1)}, u32[]{:S(2)}, u32[]{:S(2)}) collective-permute-start(bf16[3,12672]{1,0:T(4,128)(2,1)S(1)} %get-tuple-element.10), channel_id=1, source_target_pairs={{0,1},{1,2},{2,3},{3,4},{4,5},{5,6},{6,7},{7,8},{8,9},{9,10},{10,1... | collective-permute-start | bytes 228104 | tf_op jit(solution)/shard_map/ppermute | solution.py:258
  251.2 9.6 %collective-permute-start.1 = (bf16[3,12672]{1,0:T(4,128)(2,1)S(1)}, bf16[3,12672]{1,0:T(4,128)(2,1)S(1)}, u32[]{:S(2)}, u32[]{:S(2)}) collective-permute-start(bf16[3,12672]{1,0:T(4,128)(2,1)S(1)} %get-tuple-element.11), channel_id=1, source_target_pairs={{1,0},{2,1},{3,2},{4,3},{5,4},{6,5},{7,6},{8,7},{9,8},{10,9},{11,1... | collective-permute-start | bytes 228104 | tf_op jit(solution)/shard_map/ppermute | solution.py:259

commit v2 on v1

--- a/solution.py
+++ b/solution.py
@@ -12,7 +12,7 @@
 MESH = pl.DeviceIdType.MESH
 
 
-def exchange_kernel(members, slots, send_ref, recv_ref, send_sem, recv_sem, own_sem):
+def exchange_kernel(members, slots, spill, send_ref, recv_ref, send_sem, recv_sem, own_sem, *sems):
     me = lax.axis_index("member")
     barrier = pltpu.get_barrier_semaphore()
 
@@ -25,11 +25,14 @@
     lax.fori_loop(1, members, greet, 0)
     pl.semaphore_wait(barrier, members - 1)
 
+    def block(i):
+        return pl.ds(pl.multiple_of(i * slots, 16), slots)
+
     def copy(o):
         other = lax.rem(me + o, members)
         return pltpu.make_async_remote_copy(
-            src_ref=send_ref.at[pl.ds(pl.multiple_of(other * slots, slots), slots)],
-            dst_ref=recv_ref.at[pl.ds(pl.multiple_of(me * slots, slots), slots)],
+            src_ref=send_ref.at[block(other)],
+            dst_ref=recv_ref.at[block(me)],
             send_sem=send_sem.at[o],
             recv_sem=recv_sem.at[o],
             device_id={"member": other},
@@ -44,28 +47,120 @@
         copy(o).wait()
         return carry
 
-    lax.fori_loop(1, members, start, 0)
-    mine = pl.ds(pl.multiple_of(me * slots, slots), slots)
-    own = pltpu.make_async_copy(send_ref.at[mine], recv_ref.at[mine], own_sem)
-    own.start()
+    own = pltpu.make_async_copy(send_ref.at[block(me)], recv_ref.at[block(me)], own_sem.at[0])
+    if spill:
+        chain_send, chain_recv, twin_send, twin_recv = sems
+        chips = members // 2
+        chip, core = me // 2, me % 2
+        last = pl.ds(members * slots, spill)
+
+        def shelf(origin, side):
+            at = members * slots + (origin * 2 + side) * spill
+            return recv_ref.at[pl.ds(pl.multiple_of(at, 16), spill)]
+
+        def hop(origin, step, src):
+            return pltpu.make_async_remote_copy(
+                src_ref=src,
+                dst_ref=shelf(origin, core),
+                send_sem=chain_send.at[origin, (step + 1) // 2],
+                recv_sem=chain_recv.at[origin],
+                device_id={"member": lax.rem(me + 2 * step + members, members)},
+                device_id_type=MESH,
+            )
+
+        def twin(origin, src):
+            return pltpu.make_async_remote_copy(
+                src_ref=src,
+                dst_ref=shelf(origin, core),
+                send_sem=twin_send.at[origin],
+                recv_sem=twin_recv.at[origin],
+                device_id={"member": chip * 2 + 1 - core},
+                device_id_type=MESH,
+            )
+
+        own_last = pltpu.make_async_copy(send_ref.at[last], shelf(chip, core), own_sem.at[1])
+
+        def has(step):
+            return jnp.logical_and(chip + step >= 0, chip + step < chips)
+
+        for step in (1, -1):
+
+            @pl.when(has(step))
+            def _():
+                hop(chip, step, send_ref.at[last]).start()
+
+        twin(chip, send_ref.at[last]).start()
+        own_last.start()
+        lax.fori_loop(1, members, start, 0)
+        own.start()
+        for far in range(1, chips):
+            for step in (1, -1):
+                origin = chip - step * far
+
+                @pl.when(has(-step * far))
+                def _():
+                    held = shelf(origin, core)
+                    hop(origin, step, held).wait_recv()
+                    twin(origin, held).start()
+
+                    @pl.when(has(step))
+                    def _():
+                        hop(origin, step, held).start()
+
+        own_last.wait()
+        twin(chip, send_ref.at[last]).wait_send()
+        twin(chip, shelf(chip, 1 - core)).wait_recv()
+        for step in (1, -1):
+
+            @pl.when(has(step))
+            def _():
+                hop(chip, step, send_ref.at[last]).wait_send()
+
+        for far in range(1, chips):
+            for step in (1, -1):
+                origin = chip - step * far
+
+                @pl.when(has(-step * far))
+                def _():
+                    held = shelf(origin, core)
+                    twin(origin, held).wait_send()
+                    pltpu.make_async_remote_copy(
+                        src_ref=held,
+                        dst_ref=shelf(origin, 1 - core),
+                        send_sem=twin_send.at[origin],
+                        recv_sem=twin_recv.at[origin],
+                        device_id={"member": chip * 2 + 1 - core},
+                        device_id_type=MESH,
+                    ).wait_recv()
+
+                    @pl.when(has(step))
+                    def _():
+                        hop(origin, step, held).wait_send()
+
+    else:
+        lax.fori_loop(1, members, start, 0)
+        own.start()
     own.wait()
     lax.fori_loop(1, members, finish, 0)
 
 
-def exchange(send, members, slots):
+def exchange(send, members, slots, spill, total):
     width = send.shape[1]
+    dma = pltpu.SemaphoreType.DMA
+    sems = [dma((members,)), dma((members,)), dma((2,))]
+    if spill:
+        chips = members // 2
+        sems += [dma((chips, 2)), dma((chips,)), dma((chips,)), dma((chips,))]
     return pl.pallas_call(
-        functools.partial(exchange_kernel, members, slots),
-        out_shape=jax.ShapeDtypeStruct((members * slots + 16, width), send.dtype),
+        functools.partial(exchange_kernel, members, slots, spill),
+        out_shape=jax.ShapeDtypeStruct((total, width), send.dtype),
         in_specs=[pl.BlockSpec(memory_space=pl.ANY)],
         out_specs=pl.BlockSpec(memory_space=pl.ANY),
-        scratch_shapes=[
-            pltpu.SemaphoreType.DMA((members,)),
-            pltpu.SemaphoreType.DMA((members,)),
-            pltpu.SemaphoreType.DMA,
-        ],
-        compiler_params=pltpu.CompilerParams(collective_id=0, has_side_effects=True),
-        name="exchange_rows",
+        scratch_shapes=sems,
+        compiler_params=pltpu.CompilerParams(
+            collective_id=1 if spill else 0, has_side_effects=True
+        ),
+        name="exchange_spill" if spill else "exchange_rows",
     )(send)
 
 
@@ -78,15 +173,15 @@
     return x
 
 
-def setup_kernel(a_ref, p_ref, dg_ref, s_ref, co_ref, p3, s3, ap3, dinv):
-    modes, tile, width = p_ref.shape
+def setup_kernel(ext_ref, dg_ref, s_ref, co_ref, p3, s3, ap3, dinv):
+    _, modes, tile, width = s_ref.shape
     f32 = jnp.float32
     half = tile // 2
     parts = [(i, l) for l in range(width // LANES) for i in range(2)]
     diag = dg_ref[...]
     dinv[...] = jnp.where(diag > 1.0, 1.0 / jnp.where(diag > 1.0, diag, 1.0), 0.0)
     for c in range(modes):
-        own = p_ref[c].astype(f32)
+        own = ext_ref[pl.ds((3 * tile + c) * tile, tile), :].astype(f32)
         for k in range(3):
             p3[k, c] = shifted(own, k)
 
@@ -99,7 +194,8 @@
             for k in ks:
                 vecs = [ref[pl.ds(j0, 8), lanes] for ref in rows(k)]
                 for jj in range(8):
-                    a = a_ref[k, j0 + jj, pl.ds(i0, half), lanes].astype(f32)
+                    at = pl.multiple_of((k * tile + j0 + jj) * tile + i0, half)
+                    a = ext_ref[pl.ds(at, half), lanes].astype(f32)
                     for c in range(modes):
                         accs[c] = accs[c] + a * vecs[c][jj : jj + 1]
             return tuple(accs)
@@ -184,8 +280,8 @@
         lax.fori_loop(0, modes * (width // LANES), coarse, 0)
 
 
-def setup(a, p, diag):
-    modes, tile, width = p.shape
+def setup(ext, diag, modes, tile):
+    width = ext.shape[1]
     f32 = jnp.float32
     return pl.pallas_call(
         setup_kernel,
@@ -193,7 +289,7 @@
             jax.ShapeDtypeStruct((3, modes, tile, width), jnp.bfloat16),
             jax.ShapeDtypeStruct((7, modes, modes, width), f32),
         ),
-        in_specs=[pl.BlockSpec(memory_space=pltpu.VMEM)] * 3,
+        in_specs=[pl.BlockSpec(memory_space=pltpu.VMEM)] * 2,
         out_specs=(pl.BlockSpec(memory_space=pltpu.VMEM),) * 2,
         scratch_shapes=[
             pltpu.VMEM((3, modes, tile, width), f32),
@@ -203,11 +299,12 @@
         ],
         compiler_params=pltpu.CompilerParams(vmem_limit_bytes=56 * 1024 * 1024),
         name="coarse_setup",
-    )(a, p, diag)
+    )(ext, diag)
 
 
 def per_device(a_band, p_tent, new_owner):
     members = lax.axis_size("member")
+    groups = lax.axis_size("group")
     me = lax.axis_index("member")
     rows, _, tile, _ = a_band.shape
     modes = p_tent.shape[1]
@@ -216,16 +313,20 @@
     bf16, i32 = jnp.bfloat16, jnp.int32
     size = 3 * tile * tile
     width = -(-(rows + 2 * HALO) // LANES) * LANES
+    spill = 16 if slots > 32 and members % 2 == 0 else 0
+    few = slots - spill
+    total = max(members * slots, members * (few + spill))
 
     onehot = (new_owner[None, :] == jnp.arange(members, dtype=i32)[:, None]).astype(i32)
     earlier = (jnp.arange(rows)[:, None] < jnp.arange(rows)[None, :]).astype(jnp.float32)
     before = jnp.dot(onehot.astype(jnp.float32), earlier).astype(i32)
     place = jnp.sum(before * onehot, 0)
     counts = jnp.sum(onehot, 1)
-    got = lax.all_gather(counts, "member")[:, me]
-
-    flat_slot = new_owner * slots + place
-    pick = (jnp.arange(members * slots, dtype=i32)[:, None] == flat_slot[None, :]).astype(bf16)
+    axes = ("group", "member")
+    every = lax.all_gather(counts, axes)
+    table = lax.dynamic_slice_in_dim(every, lax.axis_index("group") * members, members, 0)
+    got = lax.dynamic_index_in_dim(table, me, 1, keepdims=False)
+
     dense = jnp.concatenate(
         [
             a_band.transpose(1, 3, 2, 0).reshape(size, rows),
@@ -233,26 +334,63 @@
         ],
         0,
     )
-    send = lax.dot_general(
-        pick, dense, (((1,), (1,)), ((), ())), preferred_element_type=jnp.float32
-    ).astype(bf16)
-    recv = exchange(send, members, slots)
-
-    ends = jnp.sum(
-        jnp.where(jnp.arange(members)[None, :] <= jnp.arange(members)[:, None], got[None, :], 0), 1
-    )
-    starts = ends - got
-    within = jnp.arange(slots, dtype=i32)
-    lands = jnp.where(within[None, :] < got[:, None], starts[:, None] + within[None, :], -width)
-    lands = lands.reshape(-1)
+    member = jnp.arange(members)
+    upto = member[None, :] <= member[:, None]
+    starts = jnp.sum(jnp.where(upto, got[None, :], 0), 1) - got
+
+    def sorted_send(flat_slot, count):
+        pick = (jnp.arange(count, dtype=i32)[:, None] == flat_slot[None, :]).astype(bf16)
+        return lax.dot_general(
+            pick, dense, (((1,), (1,)), ((), ())), preferred_element_type=jnp.float32
+        ).astype(bf16)
+
+    def direct(_):
+        send = sorted_send(new_owner * slots + place, members * slots)
+        return exchange(send, members, slots, 0, total + 16)
+
+    def direct_lands():
+        within = jnp.arange(slots, dtype=i32)
+        lands = jnp.where(within[None, :] < got[:, None], starts[:, None] + within[None, :], -width)
+        return jnp.pad(lands.reshape(-1), (0, total - members * slots), constant_values=-width)
+
+    if spill:
+        over = jnp.maximum(every - few, 0)
+        fits = jnp.max(jnp.sum(over, 1)) <= spill
+
+        def spilled(_):
+            mine = jnp.maximum(counts - few, 0)
+            first = jnp.sum(jnp.where(upto, mine[None, :], 0), 1) - mine
+            base = jnp.sum(first[:, None] * onehot, 0)
+            slot = jnp.where(
+                place < few, new_owner * few + place, members * few + base + place - few
+            )
+            send = sorted_send(slot, members * few + spill)
+            return exchange(send, members, few, spill, total + 16)
+
+        def spilled_lands():
+            within = jnp.arange(few, dtype=i32)
+            head = jnp.where(
+                within[None, :] < got[:, None], starts[:, None] + within[None, :], -width
+            )
+            over_group = jnp.maximum(table - few, 0)
+            before_me = jnp.sum(jnp.where(member[None, :] < me, over_group, 0), 1)
+            at = jnp.arange(spill, dtype=i32)[None, :] - before_me[:, None]
+            good = jnp.logical_and(at >= 0, at < jnp.maximum(got - few, 0)[:, None])
+            tail = jnp.where(good, starts[:, None] + few + at, -width)
+            lands = jnp.concatenate([head.reshape(-1), tail.reshape(-1)])
+            return jnp.pad(lands, (0, total - members * (few + spill)), constant_values=-width)
+
+        lands = jnp.where(fits, spilled_lands(), direct_lands())
+        recv = lax.cond(fits, spilled, direct, 0)
+    else:
+        lands = direct_lands()
+        recv = direct(0)
+
     edge = jnp.arange(16, dtype=i32)
     edge_row = jnp.where(edge < HALO, edge, jnp.where(edge < 2 * HALO, rows - 2 * HALO + edge, -1))
     rim_pick = (edge_row[:, None] == lands[None, :]).astype(bf16)
-    rim = jnp.dot(
-        rim_pick, recv[: members * slots], preferred_element_type=jnp.float32
-    ).astype(bf16)
-    axes = ("group", "member")
-    devices = lax.axis_size("group") * members
+    rim = jnp.dot(rim_pick, recv[:total], preferred_element_type=jnp.float32).astype(bf16)
+    devices = groups * members
     up = [(i, i + 1) for i in range(devices - 1)]
     down = [(i + 1, i) for i in range(devices - 1)]
     from_left = lax.ppermute(rim[HALO : 2 * HALO], axes, up)
@@ -260,18 +398,17 @@
     halo = jnp.concatenate(
         [from_left, from_right, jnp.zeros((16 - 2 * HALO, rim.shape[1]), bf16)], 0
     )
-    recv = lax.dynamic_update_slice(recv, halo, (members * slots, 0))
+    recv = lax.dynamic_update_slice(recv, halo, (total, 0))
     halo_lane = jnp.where(edge < HALO, edge, jnp.where(edge < 2 * HALO, rows + edge, -1))
     lane = jnp.concatenate([lands + HALO, halo_lane])
     place_out = (lane[:, None] == jnp.arange(width, dtype=i32)[None, :]).astype(bf16)
     ext = lax.dot_general(
         recv, place_out, (((0,), (0,)), ((), ())), preferred_element_type=jnp.float32
     ).astype(bf16)
-    a = ext[:size].reshape(3, tile, tile, width)
-    p = ext[size:].reshape(modes, tile, width)
+    centre = ext[tile * tile : 2 * tile * tile].reshape(tile, tile, width)
     eye = jnp.eye(tile, dtype=bf16)[:, :, None]
-    diag = jnp.sum((a[1] * eye).astype(jnp.float32), 0)
-    s_out, co = setup(a, p, diag)
+    diag = jnp.sum((centre * eye).astype(jnp.float32), 0)
+    s_out, co = setup(ext, diag, modes, tile)
     p_smooth = s_out[..., HALO : HALO + rows].transpose(3, 0, 1, 2)
     coarse = co[..., HALO : HALO + rows].reshape(7 * modes * modes, rows).T
     return (p_smooth, coarse)

time: 313 us -> 316 us (level)
  Pallas kernels: 254 us -> 213 us
  blocking collectives: 4.24 us -> 38.2 us
  other arithmetic: 2.75 us -> 17.6 us
  local copies, waits for them, and re-layouts: 19.1 us -> 12.4 us
    pallas_call x1, Pallas kernels: 216 us -> 175 us  [exchange(): pl.pallas_call(functools.partial(exchange_kernel, members, slots, spill),...]
    unnamed x1, blocking collectives: 4.24 us -> 38.2 us
    concatenate x0 -> x1, other arithmetic: none -> 12.4 us  [per_device(): jnp.concatenate([a_band.transpose(1, 3, 2, 0).reshape(size, rows), p_tent...]
    slice x3 -> x1, local copies, waits for them, and re-layouts: 3.8 us -> 0.14 us  [per_device(): centre = ext[tile * tile:2 * tile * tile].reshape(tile, tile, width)]
where the time goes in v2:
time: 316 us; the launch traced here: 315 us
  Pallas kernels  213 us (67%)
  blocking collectives  38.2 us (12%)
  matrix products  18 us (6%)
  other arithmetic  17.6 us (6%)
  local copies, waits for them, and re-layouts  12.4 us (4%)
  waiting for transfers between devices  7.51 us (2%)
  starting transfers between devices  6.22 us (2%)
    pallas_call x1, Pallas kernels, exchange(): pl.pallas_call(functools.partial(exchange_kernel, members, slots, spill),...  175 us
    pallas_call x1, Pallas kernels, setup(): pl.pallas_call(setup_kernel, out_shape=(jax.ShapeDtypeStruct((3, modes, t...  38.3 us
    unnamed x1, blocking collectives  38.2 us
    concatenate x1, other arithmetic, per_device(): jnp.concatenate([a_band.transpose(1, 3, 2, 0).reshape(size, rows), p_tent...  12.4 us
    dot_general x1, matrix products, sorted_send(): lax.dot_general(pick, dense, (((1,), (1,)), ((), ())), preferred_element_...  7.63 us
    ppermute x1, waiting for transfers between devices, per_device(): from_right = lax.ppermute(rim[:HALO], axes, down)  7.51 us
    transpose x1, local copies, waits for them, and re-layouts, per_device(): a_band.transpose(1, 3, 2, 0).reshape(size, rows)  6.39 us
  transfers between devices with their start and end apart: 2, of which 1 were waited for; matrix products, arithmetic and copies ran while one was open for 0% of the time, Pallas kernels for 0%

profile of v2, /device:TPU:27, one launch (start us, length us, event | category | flops | bytes accessed | tf_op | source)
XLA Modules:
  0.0 315.2 jit_solution(14439373073350265504)
XLA Ops:
  0.6 0.0 copy-start.2
  0.7 0.8 fusion.14
  1.5 0.2 dynamic-update-slice
  1.8 38.2 %all-reduce = s32[256]{0:T(256)S(1)} all-reduce(s32[256]{0:T(256)S(1)} %dynamic-update-slice), channel_id=2, replica_groups=mesh['group'=4,'member'=8] {'group','member'}, use_global_device_ids=true, to_apply=%add | all-reduce | flops 256 | bytes 2048
  39.9 0.1 reshape.131
  40.0 0.2 dynamic-slice_reduce_fusion
  40.2 0.1 select_reduce_fusion.2
  40.3 0.1 copy.12
  40.4 0.2 add_reduce_fusion
  40.7 0.1 add_select_fusion
  40.7 0.1 add_select_fusion.2
  40.8 0.1 maximum_reduce_fusion
  40.9 0.9 fusion.5
  41.8 0.7 fusion.12
  42.5 0.1 select_reduce_fusion.1
  42.7 0.1 add_select_fusion.1
  42.7 0.1 select_n.104
  42.8 0.1 select_n.106
  42.9 0.1 select_n.101
  43.0 0.6 reduce_max.9
  44.3 6.4 %copy.11 = bf16[3,64,64,192]{3,2,1,0:T(8,128)(2,1)S(1)} copy(bf16[3,64,64,192]{3,1,2,0:T(8,128)(2,1)} %bitcast.15) | data formatting | bytes 9437184 | tf_op jit(solution)/shard_map/transpose | solution.py:332
  50.7 0.0 copy-start.3
  50.7 0.0 copy-done.2
  50.7 12.4 %pad_maximum_fusion = bf16[12672,192]{1,0:T(8,128)(2,1)} fusion(bf16[384,192]{1,0:T(8,128)(2,1)S(1)} %bitcast.17, bf16[12288,192]{1,0:T(8,128)(2,1)S(1)} %bitcast.13), kind=kLoop, calls=%fused_computation.15 | loop fusion | flops 9732096 | bytes 9732096 | tf_op jit(solution)/shard_map/concatenate | solution.py:330
  63.1 0.0 copy-done.3
  63.1 183.3 %conditional.1 = (bf16[400,12672]{1,0:T(8,128)(2,1)}) conditional(s32[]{:T(128)} %convert_element_type.40, (s32[192]{0:T(256)S(1)}, s32[192]{0:T(256)S(1)}, bf16[12672,192]{1,0:T(8,128)(2,1)}) %tuple.36, (s32[192]{0:T(256)S(1)}, s32[192]{0:T(256)S(1)}, s32[8]{0:T(128)S(1)}, pred[8,8]{1,0:T(8,128)(4,1)S(1)}, s32[8,192]{1,0:T(8,128)S(1)}, ...), branch_computations={%region_4.5_spmd, %region_5.8_spmd} | conditional | flops 1873502592 | bytes 14601224 | solution.py:384
  63.3 0.1 select_reduce_fusion
  63.4 0.1 multiply_reduce_fusion
  63.5 7.6 %convolution_convert_fusion.1.send_ref = bf16[272,12672]{1,0:T(8,128)(2,1)} fusion(bf16[12672,192]{1,0:T(8,128)(2,1)} %get-tuple-element.33, s32[192]{0:T(256)S(1)} %compare_select_fusion), kind=kOutput, calls=%fused_computation.4 | convolution fusion | flops 1327064064 | bytes 11760384 | tf_op jit(solution)/shard_map/cond/branch_1_fun/dot_general | solution.py:343
  71.2 175.2 %exchange_spill.1 = bf16[400,12672]{1,0:T(8,128)(2,1)} custom-call(bf16[272,12672]{1,0:T(8,128)(2,1)} %convolution_convert_fusion.1.send_ref), custom_call_target="tpu_custom_call" | custom-call | tf_op jit(solution)/shard_map/cond/branch_1_fun/exchange_spill/pallas_call | solution.py:154
  246.4 0.0 copy-start
  246.4 5.3 %convolution_convert_fusion.3 = bf16[16,12672]{1,0:T(8,128)(2,1)S(1)} fusion(bf16[400,12672]{1,0:T(8,128)(2,1)} %get-tuple-element.57, s32[384]{0:T(512)S(1)} %get-tuple-element.54, s32[16]{0:T(128)S(1)} %compare_select_fusion.2), kind=kOutput, calls=%fused_computation.13 | convolution fusion | flops 155922432 | bytes 10139200 | tf_op jit(solution)/shard_map/dot_general | solution.py:392
  251.7 0.1 fusion.22
  251.8 4.3 %collective-permute-start = (bf16[3,12672]{1,0:T(4,128)(2,1)S(1)}, bf16[3,12672]{1,0:T(4,128)(2,1)S(1)}, u32[]{:S(2)}, u32[]{:S(2)}) collective-permute-start(bf16[3,12672]{1,0:T(4,128)(2,1)S(1)} %get-tuple-element.55), channel_id=1, source_target_pairs={{0,1},{1,2},{2,3},{3,4},{4,5},{5,6},{6,7},{7,8},{8,9},{9,10},{10,1... | collective-permute-start | bytes 228104 | tf_op jit(solution)/shard_map/ppermute | solution.py:396
  256.1 1.9 collective-permute-start.1
  258.1 0.1 pad.4.clone
  258.2 0.0 collective-permute-done
  258.2 7.5 %collective-permute-done.1 = bf16[3,12672]{1,0:T(4,128)(2,1)S(1)} collective-permute-done((bf16[3,12672]{1,0:T(4,128)(2,1)S(1)}, bf16[3,12672]{1,0:T(4,128)(2,1)S(1)}, u32[]{:S(2)}, u32[]{:S(2)}) %collective-permute-start.1) | collective-permute-done | bytes 76064 | tf_op jit(solution)/shard_map/ppermute | solution.py:397
  265.7 0.0 copy-done
  265.7 0.2 maximum_dynamic-update-slice_fusion
  265.9 4.2 %convolution_convert_fusion.2.ext_ref = bf16[12672,256]{1,0:T(8,128)(2,1)S(1)} fusion(bf16[400,12672]{1,0:T(8,128)(2,1)S(1)} %maximum_dynamic-update-slice_fusion, s32[400]{0:T(512)S(1)} %pad_add_fusion), kind=kOutput, calls=%fused_computation.12 | convolution fusion | flops 2598572032 | bytes 16627264 | tf_op jit(solution)/shard_map/dot_general | solution.py:405
  270.0 0.0 copy-start.1
  270.0 0.1 slice.32
  270.2 1.8 convert_reduce_fusion.dg_ref
  272.0 0.8 copy-done.1
  272.8 38.3 %coarse_setup.1 = (bf16[3,6,64,256]{3,2,1,0:T(8,128)(2,1)}, f32[7,6,6,256]{3,2,1,0:T(8,128)}) custom-call(bf16[12672,256]{1,0:T(8,128)(2,1)} %copy-done.1, f32[64,256]{1,0:T(8,128)} %convert_reduce_fusion.dg_ref), custom_call_target="tpu_custom_call" | custom-call | tf_op jit(solution)/shard_map/coarse_setup/pallas_call | solution.py:286
  311.1 1.1 slice.29
  312.2 0.8 copy.13
  313.0 2.1 slice_bitcast_fusion
  (13 shorter events, 0.1 us)
Async XLA Ops:
  0.6 50.0 %copy-start.2 = (bf16[192,6,64]{0,2,1:T(8,128)(2,1)S(1)}, bf16[192,6,64]{0,2,1:T(8,128)(2,1)}, u32[]{:S(2)}) copy-start(bf16[192,6,64]{0,2,1:T(8,128)(2,1)} %param.6) | copy-start | bytes 442372
  50.7 12.4 %copy-start.3 = (s32[192]{0:T(256)S(1)}, s32[192]{0:T(256)}, u32[]{:S(2)}) copy-start(s32[192]{0:T(256)} %param.7) | copy-start | bytes 2308
  246.4 19.3 %copy-start = (bf16[400,12672]{1,0:T(8,128)(2,1)S(1)}, bf16[400,12672]{1,0:T(8,128)(2,1)}, u32[]{:S(2)}) copy-start(bf16[400,12672]{1,0:T(8,128)(2,1)} %get-tuple-element.57) | copy-start | bytes 30412804
  251.8 6.4 %collective-permute-start = (bf16[3,12672]{1,0:T(4,128)(2,1)S(1)}, bf16[3,12672]{1,0:T(4,128)(2,1)S(1)}, u32[]{:S(2)}, u32[]{:S(2)}) collective-permute-start(bf16[3,12672]{1,0:T(4,128)(2,1)S(1)} %get-tuple-element.55), channel_id=1, source_target_pairs={{0,1},{1,2},{2,3},{3,4},{4,5},{5,6},{6,7},{7,8},{8,9},{9,10},{10,1... | collective-permute-start | bytes 228104 | tf_op jit(solution)/shard_map/ppermute | solution.py:396
  256.1 9.6 %collective-permute-start.1 = (bf16[3,12672]{1,0:T(4,128)(2,1)S(1)}, bf16[3,12672]{1,0:T(4,128)(2,1)S(1)}, u32[]{:S(2)}, u32[]{:S(2)}) collective-permute-start(bf16[3,12672]{1,0:T(4,128)(2,1)S(1)} %get-tuple-element.56), channel_id=1, source_target_pairs={{1,0},{2,1},{3,2},{4,3},{5,4},{6,5},{7,6},{8,7},{9,8},{10,9},{11,1... | collective-permute-start | bytes 228104 | tf_op jit(solution)/shard_map/ppermute | solution.py:397
  270.0 2.8 copy-start.1

commit v3 on v2

--- a/solution.py
+++ b/solution.py
@@ -89,10 +89,19 @@
             def _():
                 hop(chip, step, send_ref.at[last]).start()
 
+        def start_far(far):
+            for step in (1, -1):
+
+                @pl.when(has(step * far))
+                def _():
+                    for side in range(2):
+                        copy(lax.rem(members + 2 * step * far + side - core, members)).start()
+
         twin(chip, send_ref.at[last]).start()
+        copy(lax.rem(members + 1 - 2 * core, members)).start()
         own_last.start()
-        lax.fori_loop(1, members, start, 0)
         own.start()
+        start_far(1)
         for far in range(1, chips):
             for step in (1, -1):
                 origin = chip - step * far
@@ -106,6 +115,9 @@
                     @pl.when(has(step))
                     def _():
                         hop(origin, step, held).start()
+
+            if far + 1 < chips:
+                start_far(far + 1)
 
         own_last.wait()
         twin(chip, send_ref.at[last]).wait_send()
@@ -162,6 +174,59 @@
         ),
         name="exchange_spill" if spill else "exchange_rows",
     )(send)
+
+
+def counts_kernel(groups, members, own_ref, all_ref, send_sem, recv_sem):
+    devices = groups * members
+    flat = lax.axis_index("group") * members + lax.axis_index("member")
+    barrier = pltpu.get_barrier_semaphore()
+
+    def target(o):
+        other = lax.rem(flat + o, devices)
+        return {"group": other // members, "member": lax.rem(other, members)}
+
+    def greet(o, carry):
+        pl.semaphore_signal(barrier, inc=1, device_id=target(o), device_id_type=MESH)
+        return carry
+
+    lax.fori_loop(1, devices, greet, 0)
+    pl.semaphore_wait(barrier, devices - 1)
+
+    def copy(o):
+        return pltpu.make_async_remote_copy(
+            src_ref=own_ref,
+            dst_ref=all_ref.at[flat],
+            send_sem=send_sem.at[o],
+            recv_sem=recv_sem.at[o],
+            device_id=target(o),
+            device_id_type=MESH,
+        )
+
+    def start(o, carry):
+        copy(o).start()
+        return carry
+
+    def finish(o, carry):
+        copy(o).wait()
+        return carry
+
+    lax.fori_loop(1, devices, start, 0)
+    all_ref[flat] = own_ref[...]
+    lax.fori_loop(1, devices, finish, 0)
+
+
+def share_counts(counts, groups, members):
+    devices = groups * members
+    own = jnp.pad(counts, (0, LANES - members))[None, :]
+    return pl.pallas_call(
+        functools.partial(counts_kernel, groups, members),
+        out_shape=jax.ShapeDtypeStruct((devices, 1, LANES), counts.dtype),
+        in_specs=[pl.BlockSpec(memory_space=pltpu.VMEM)],
+        out_specs=pl.BlockSpec(memory_space=pltpu.VMEM),
+        scratch_shapes=[pltpu.SemaphoreType.DMA((devices,))] * 2,
+        compiler_params=pltpu.CompilerParams(collective_id=2, has_side_effects=True),
+        name="share_counts",
+    )(own)[:, 0, :members]
 
 
 def shifted(x, k):
@@ -323,8 +388,11 @@
     place = jnp.sum(before * onehot, 0)
     counts = jnp.sum(onehot, 1)
     axes = ("group", "member")
-    every = lax.all_gather(counts, axes)
-    table = lax.dynamic_slice_in_dim(every, lax.axis_index("group") * members, members, 0)
+    if spill:
+        every = share_counts(counts, groups, members)
+        table = lax.dynamic_slice_in_dim(every, lax.axis_index("group") * members, members, 0)
+    else:
+        table = lax.all_gather(counts, "member")
     got = lax.dynamic_index_in_dim(table, me, 1, keepdims=False)
 
     dense = jnp.concatenate(
@@ -344,8 +412,9 @@
             pick, dense, (((1,), (1,)), ((), ())), preferred_element_type=jnp.float32
         ).astype(bf16)
 
-    def direct(_):
-        send = sorted_send(new_owner * slots + place, members * slots)
+    flat_slot = new_owner * slots + place
+
+    def direct(send):
         return exchange(send, members, slots, 0, total + 16)
 
     def direct_lands():
@@ -357,14 +426,14 @@
         over = jnp.maximum(every - few, 0)
         fits = jnp.max(jnp.sum(over, 1)) <= spill
 
-        def spilled(_):
-            mine = jnp.maximum(counts - few, 0)
-            first = jnp.sum(jnp.where(upto, mine[None, :], 0), 1) - mine
-            base = jnp.sum(first[:, None] * onehot, 0)
-            slot = jnp.where(
-                place < few, new_owner * few + place, members * few + base + place - few
-            )
-            send = sorted_send(slot, members * few + spill)
+        mine = jnp.maximum(counts - few, 0)
+        first = jnp.sum(jnp.where(upto, mine[None, :], 0), 1) - mine
+        base = jnp.sum(first[:, None] * onehot, 0)
+        spill_slot = jnp.where(
+            place < few, new_owner * few + place, members * few + base + place - few
+        )
+
+        def spilled(send):
             return exchange(send, members, few, spill, total + 16)
 
         def spilled_lands():
@@ -381,10 +450,11 @@
             return jnp.pad(lands, (0, total - members * (few + spill)), constant_values=-width)
 
         lands = jnp.where(fits, spilled_lands(), direct_lands())
-        recv = lax.cond(fits, spilled, direct, 0)
+        send = sorted_send(jnp.where(fits, spill_slot, flat_slot), members * slots)
+        recv = lax.cond(fits, spilled, direct, send)
     else:
         lands = direct_lands()
-        recv = direct(0)
+        recv = direct(sorted_send(flat_slot, members * slots))
 
     edge = jnp.arange(16, dtype=i32)
     edge_row = jnp.where(edge < HALO, edge, jnp.where(edge < 2 * HALO, rows - 2 * HALO + edge, -1))

time: 316 us -> 276 us (0.87)
  blocking collectives: 38.2 us -> 0 us
  other arithmetic: 17.6 us -> 6.29 us
  Pallas kernels: 213 us -> 219 us
    unnamed x1 -> x0, blocking collectives: 38.2 us -> none
    concatenate x1 -> x0, other arithmetic: 12.4 us -> none  [per_device(): jnp.concatenate([a_band.transpose(1, 3, 2, 0).reshape(size, rows), p_tent...]
    pallas_call x0 -> x1, Pallas kernels: none -> 9.25 us  [share_counts(): pl.pallas_call(functools.partial(counts_kernel, groups, members), out_sha...]
    pallas_call x1, Pallas kernels: 175 us -> 172 us  [exchange(): pl.pallas_call(functools.partial(exchange_kernel, members, slots, spill),...]
where the time goes in v3:
time: 276 us
  Pallas kernels  219 us (79%)
  matrix products  19.7 us (7%)
  local copies, waits for them, and re-layouts  15.3 us (6%)
  waiting for transfers between devices  7.33 us (3%)
  other arithmetic  6.29 us (2%)
  starting transfers between devices  6.22 us (2%)
    pallas_call x1, Pallas kernels, exchange(): pl.pallas_call(functools.partial(exchange_kernel, members, slots, spill),...  172 us
    pallas_call x1, Pallas kernels, setup(): pl.pallas_call(setup_kernel, out_shape=(jax.ShapeDtypeStruct((3, modes, t...  38.3 us
    dot_general x1, matrix products, sorted_send(): lax.dot_general(pick, dense, (((1,), (1,)), ((), ())), preferred_element_...  9.27 us
    pallas_call x1, Pallas kernels, share_counts(): pl.pallas_call(functools.partial(counts_kernel, groups, members), out_sha...  9.25 us
    transpose x1, local copies, waits for them, and re-layouts, per_device(): a_band.transpose(1, 3, 2, 0).reshape(size, rows)  9.05 us
    ppermute x1, waiting for transfers between devices, per_device(): from_right = lax.ppermute(rim[:HALO], axes, down)  7.33 us
  transfers between devices with their start and end apart: 2, of which 1 were waited for; matrix products, arithmetic and copies ran while one was open for 0% of the time, Pallas kernels for 0%

profile of v3, /device:TPU:27, one launch (start us, length us, event | category | flops | bytes accessed | tf_op | source)
XLA Modules:
  0.0 275.8 jit_solution(10975277422455590043)
XLA Ops:
  0.6 0.0 copy-start.2
  0.6 0.0 copy-start.3
  0.7 0.9 convert_reduce_fusion.1
  1.5 0.5 pad_bitcast_fusion.own_ref
  2.0 9.2 %share_counts.1 = s32[32,1,128]{2,1,0:T(1,128)} custom-call(s32[1,128]{1,0:T(1,128)} %pad_bitcast_fusion.own_ref), custom_call_target="tpu_custom_call" | custom-call | tf_op jit(solution)/shard_map/share_counts/pallas_call | solution.py:221
  11.3 1.4 fusion.22
  12.7 0.3 dynamic-slice_reduce_fusion
  13.0 0.1 select_reduce_fusion.2
  13.2 0.1 add_select_fusion
  13.2 0.1 add_select_fusion.2
  13.3 0.9 fusion.5
  14.2 0.1 select_reduce_fusion.1
  14.4 0.1 add_select_fusion.1
  14.4 0.1 select_n.116
  14.5 0.1 select_n.118
  14.6 0.1 select_n.113
  14.7 0.1 select_reduce_fusion.3
  14.8 0.8 select_reduce_fusion
  15.6 9.1 %copy.6 = bf16[3,64,64,192]{3,2,1,0:T(8,128)(2,1)} copy(bf16[3,64,64,192]{3,1,2,0:T(8,128)(2,1)} %bitcast.14) | data formatting | bytes 9437184 | tf_op jit(solution)/shard_map/transpose | solution.py:400
  24.6 0.6 reduce_max.9
  25.9 0.0 copy-done.2
  25.9 0.0 copy-done.3
  25.9 9.3 %convolution_convert_fusion = bf16[384,12672]{1,0:T(8,128)(2,1)} fusion(bf16[384,192]{1,0:T(8,128)(2,1)S(1)} %bitcast.18, bf16[12288,192]{1,0:T(8,128)(2,1)} %bitcast.15, s32[192]{0:T(256)S(1)} %fusion.18), kind=kOutput, calls=%fused_computation | convolution fusion | flops 1883234304 | bytes 14598912 | tf_op jit(solution)/shard_map/dot_general | solution.py:411
  35.2 172.0 %conditional.1 = (bf16[400,12672]{1,0:T(8,128)(2,1)}) conditional(s32[]{:T(128)} %convert_element_type.42, bf16[384,12672]{1,0:T(8,128)(2,1)} %convolution_convert_fusion, bf16[384,12672]{1,0:T(8,128)(2,1)} %convolution_convert_fusion), branch_computations={%region_6.7_spmd, %region_7.8_spmd} | conditional | bytes 8 | solution.py:454
  35.2 172.0 %exchange_spill.1 = bf16[400,12672]{1,0:T(8,128)(2,1)} custom-call(bf16[384,12672]{1,0:T(8,128)(2,1)} %send_ref.1), custom_call_target="tpu_custom_call" | custom-call | tf_op jit(solution)/shard_map/cond/branch_1_fun/exchange_spill/pallas_call | solution.py:166
  207.2 0.0 copy-start
  207.2 5.3 %convolution_convert_fusion.2 = bf16[16,12672]{1,0:T(8,128)(2,1)S(1)} fusion(bf16[400,12672]{1,0:T(8,128)(2,1)} %get-tuple-element.27, s32[384]{0:T(512)S(1)} %get-tuple-element.18, s32[16]{0:T(128)S(1)} %compare_select_fusion.1), kind=kOutput, calls=%fused_computation.2 | convolution fusion | flops 155922432 | bytes 10139200 | tf_op jit(solution)/shard_map/dot_general | solution.py:462
  212.5 0.1 fusion.21
  212.6 4.1 %collective-permute-start = (bf16[3,12672]{1,0:T(4,128)(2,1)S(1)}, bf16[3,12672]{1,0:T(4,128)(2,1)S(1)}, u32[]{:S(2)}, u32[]{:S(2)}) collective-permute-start(bf16[3,12672]{1,0:T(4,128)(2,1)S(1)} %get-tuple-element.21), channel_id=1, source_target_pairs={{0,1},{1,2},{2,3},{3,4},{4,5},{5,6},{6,7},{7,8},{8,9},{9,10},{10,1... | collective-permute-start | bytes 228104 | tf_op jit(solution)/shard_map/ppermute | solution.py:466
  216.8 2.1 collective-permute-start.1
  218.9 0.1 pad.9.clone
  219.0 0.0 collective-permute-done
  219.0 7.3 %collective-permute-done.1 = bf16[3,12672]{1,0:T(4,128)(2,1)S(1)} collective-permute-done((bf16[3,12672]{1,0:T(4,128)(2,1)S(1)}, bf16[3,12672]{1,0:T(4,128)(2,1)S(1)}, u32[]{:S(2)}, u32[]{:S(2)}) %collective-permute-start.1) | collective-permute-done | bytes 76064 | tf_op jit(solution)/shard_map/ppermute | solution.py:467
  226.3 0.0 copy-done
  226.3 0.2 maximum_dynamic-update-slice_fusion
  226.5 4.2 %convolution_convert_fusion.1.ext_ref = bf16[12672,256]{1,0:T(8,128)(2,1)S(1)} fusion(bf16[400,12672]{1,0:T(8,128)(2,1)S(1)} %maximum_dynamic-update-slice_fusion, s32[400]{0:T(512)S(1)} %pad_add_fusion), kind=kOutput, calls=%fused_computation.1 | convolution fusion | flops 2598572032 | bytes 16627264 | tf_op jit(solution)/shard_map/dot_general | solution.py:475
  230.7 0.0 copy-start.1
  230.7 0.1 slice.36
  230.8 1.8 convert_reduce_fusion.dg_ref
  232.6 0.8 copy-done.1
  233.4 38.3 %coarse_setup.1 = (bf16[3,6,64,256]{3,2,1,0:T(8,128)(2,1)}, f32[7,6,6,256]{3,2,1,0:T(8,128)}) custom-call(bf16[12672,256]{1,0:T(8,128)(2,1)} %copy-done.1, f32[64,256]{1,0:T(8,128)} %convert_reduce_fusion.dg_ref), custom_call_target="tpu_custom_call" | custom-call | tf_op jit(solution)/shard_map/coarse_setup/pallas_call | solution.py:351
  271.7 1.1 slice.33
  272.9 0.8 copy.7
  273.7 2.1 slice_bitcast_fusion
  (12 shorter events, 0.1 us)
Async XLA Ops:
  0.6 25.3 %copy-start.2 = (s32[192]{0:T(256)S(1)}, s32[192]{0:T(256)}, u32[]{:S(2)}) copy-start(s32[192]{0:T(256)} %param.7) | copy-start | bytes 2308
  0.6 25.3 %copy-start.3 = (bf16[192,6,64]{0,2,1:T(8,128)(2,1)S(1)}, bf16[192,6,64]{0,2,1:T(8,128)(2,1)}, u32[]{:S(2)}) copy-start(bf16[192,6,64]{0,2,1:T(8,128)(2,1)} %param.6) | copy-start | bytes 442372
  207.2 19.1 %copy-start = (bf16[400,12672]{1,0:T(8,128)(2,1)S(1)}, bf16[400,12672]{1,0:T(8,128)(2,1)}, u32[]{:S(2)}) copy-start(bf16[400,12672]{1,0:T(8,128)(2,1)} %get-tuple-element.27) | copy-start | bytes 30412804
  212.6 6.4 %collective-permute-start = (bf16[3,12672]{1,0:T(4,128)(2,1)S(1)}, bf16[3,12672]{1,0:T(4,128)(2,1)S(1)}, u32[]{:S(2)}, u32[]{:S(2)}) collective-permute-start(bf16[3,12672]{1,0:T(4,128)(2,1)S(1)} %get-tuple-element.21), channel_id=1, source_target_pairs={{0,1},{1,2},{2,3},{3,4},{4,5},{5,6},{6,7},{7,8},{8,9},{9,10},{10,1... | collective-permute-start | bytes 228104 | tf_op jit(solution)/shard_map/ppermute | solution.py:466
  216.8 9.6 %collective-permute-start.1 = (bf16[3,12672]{1,0:T(4,128)(2,1)S(1)}, bf16[3,12672]{1,0:T(4,128)(2,1)S(1)}, u32[]{:S(2)}, u32[]{:S(2)}) collective-permute-start(bf16[3,12672]{1,0:T(4,128)(2,1)S(1)} %get-tuple-element.22), channel_id=1, source_target_pairs={{1,0},{2,1},{3,2},{4,3},{5,4},{6,5},{7,6},{8,7},{9,8},{10,9},{11,1... | collective-permute-start | bytes 228104 | tf_op jit(solution)/shard_map/ppermute | solution.py:467
  230.7 2.8 copy-start.1

commit v4 on v3

--- a/solution.py
+++ b/solution.py
@@ -12,7 +12,10 @@
 MESH = pl.DeviceIdType.MESH
 
 
-def exchange_kernel(members, slots, spill, send_ref, recv_ref, send_sem, recv_sem, own_sem, *sems):
+def exchange_kernel(
+    members, slots, spill, step_lanes, pick_ref, a_ref, p_ref, recv_ref, send_ref, blank_ref,
+    blank_sem, send_sem, recv_sem, own_sem, *sems
+):
     me = lax.axis_index("member")
     barrier = pltpu.get_barrier_semaphore()
 
@@ -23,110 +26,155 @@
         return carry
 
     lax.fori_loop(1, members, greet, 0)
-    pl.semaphore_wait(barrier, members - 1)
+    blank_ref[...] = jnp.zeros_like(blank_ref)
+    spare = pl.ds(recv_ref.shape[0] - 16, 16)
+    blank = pltpu.make_async_copy(blank_ref, recv_ref.at[spare], blank_sem)
+    blank.start()
+
+    steps = a_ref.shape[0] // step_lanes
+    cuts = ((0, 4), (4, steps + 1))
+
+    def gathered(rows):
+        return lax.dot_general(
+            pick_ref[...], rows, (((1,), (1,)), ((), ())), preferred_element_type=jnp.float32
+        ).astype(send_ref.dtype)
+
+    def gather(first, end):
+        def body(i, carry):
+            at = pl.ds(pl.multiple_of(i * step_lanes, step_lanes), step_lanes)
+            send_ref[:, at] = gathered(a_ref[at, :])
+            return carry
+
+        lax.fori_loop(first, min(end, steps), body, 0)
+        if end > steps:
+            send_ref[:, steps * step_lanes :] = gathered(p_ref[...])
+
+    def lanes(n):
+        return pl.ds(cuts[n][0] * step_lanes, (cuts[n][1] - cuts[n][0]) * step_lanes)
 
     def block(i):
         return pl.ds(pl.multiple_of(i * slots, 16), slots)
 
-    def copy(o):
+    def copy(n, o):
         other = lax.rem(me + o, members)
         return pltpu.make_async_remote_copy(
-            src_ref=send_ref.at[block(other)],
-            dst_ref=recv_ref.at[block(me)],
-            send_sem=send_sem.at[o],
-            recv_sem=recv_sem.at[o],
+            src_ref=send_ref.at[block(other), lanes(n)],
+            dst_ref=recv_ref.at[block(me), lanes(n)],
+            send_sem=send_sem.at[n, o],
+            recv_sem=recv_sem.at[n, o],
             device_id={"member": other},
             device_id_type=MESH,
         )
 
-    def start(o, carry):
-        copy(o).start()
-        return carry
-
-    def finish(o, carry):
-        copy(o).wait()
-        return carry
-
-    own = pltpu.make_async_copy(send_ref.at[block(me)], recv_ref.at[block(me)], own_sem.at[0])
-    if spill:
-        chain_send, chain_recv, twin_send, twin_recv = sems
-        chips = members // 2
-        chip, core = me // 2, me % 2
-        last = pl.ds(members * slots, spill)
-
-        def shelf(origin, side):
-            at = members * slots + (origin * 2 + side) * spill
-            return recv_ref.at[pl.ds(pl.multiple_of(at, 16), spill)]
-
-        def hop(origin, step, src):
-            return pltpu.make_async_remote_copy(
-                src_ref=src,
-                dst_ref=shelf(origin, core),
-                send_sem=chain_send.at[origin, (step + 1) // 2],
-                recv_sem=chain_recv.at[origin],
-                device_id={"member": lax.rem(me + 2 * step + members, members)},
-                device_id_type=MESH,
-            )
-
-        def twin(origin, src):
-            return pltpu.make_async_remote_copy(
-                src_ref=src,
-                dst_ref=shelf(origin, core),
-                send_sem=twin_send.at[origin],
-                recv_sem=twin_recv.at[origin],
-                device_id={"member": chip * 2 + 1 - core},
-                device_id_type=MESH,
-            )
-
-        own_last = pltpu.make_async_copy(send_ref.at[last], shelf(chip, core), own_sem.at[1])
-
-        def has(step):
-            return jnp.logical_and(chip + step >= 0, chip + step < chips)
-
+    def own(n):
+        return pltpu.make_async_copy(
+            send_ref.at[block(me), lanes(n)], recv_ref.at[block(me), lanes(n)], own_sem.at[n, 0]
+        )
+
+    def start_all(n):
+        def start(o, carry):
+            copy(n, o).start()
+            return carry
+
+        lax.fori_loop(1, members, start, 0)
+        own(n).start()
+
+    def finish_all(n):
+        def finish(o, carry):
+            copy(n, o).wait()
+            return carry
+
+        own(n).wait()
+        lax.fori_loop(1, members, finish, 0)
+
+    if not spill:
+        gather(*cuts[0])
+        pl.semaphore_wait(barrier, members - 1)
+        start_all(0)
+        gather(*cuts[1])
+        start_all(1)
+        finish_all(0)
+        finish_all(1)
+        blank.wait()
+        return
+
+    chain_send, chain_recv, twin_send, twin_recv = sems
+    chips = members // 2
+    chip, core = me // 2, me % 2
+
+    def last(n):
+        return send_ref.at[pl.ds(members * slots, spill), lanes(n)]
+
+    def shelf(n, origin, side):
+        at = members * slots + (origin * 2 + side) * spill
+        return recv_ref.at[pl.ds(pl.multiple_of(at, 16), spill), lanes(n)]
+
+    def hop(n, origin, step, src):
+        return pltpu.make_async_remote_copy(
+            src_ref=src,
+            dst_ref=shelf(n, origin, core),
+            send_sem=chain_send.at[n, origin, (step + 1) // 2],
+            recv_sem=chain_recv.at[n, origin],
+            device_id={"member": lax.rem(me + 2 * step + members, members)},
+            device_id_type=MESH,
+        )
+
+    def twin(n, origin, src, side):
+        return pltpu.make_async_remote_copy(
+            src_ref=src,
+            dst_ref=shelf(n, origin, side),
+            send_sem=twin_send.at[n, origin],
+            recv_sem=twin_recv.at[n, origin],
+            device_id={"member": chip * 2 + 1 - core},
+            device_id_type=MESH,
+        )
+
+    def own_last(n):
+        return pltpu.make_async_copy(last(n), shelf(n, chip, core), own_sem.at[n, 1])
+
+    def has(step):
+        return jnp.logical_and(chip + step >= 0, chip + step < chips)
+
+    def launch(n):
         for step in (1, -1):
 
             @pl.when(has(step))
             def _():
-                hop(chip, step, send_ref.at[last]).start()
-
-        def start_far(far):
-            for step in (1, -1):
-
-                @pl.when(has(step * far))
-                def _():
-                    for side in range(2):
-                        copy(lax.rem(members + 2 * step * far + side - core, members)).start()
-
-        twin(chip, send_ref.at[last]).start()
-        copy(lax.rem(members + 1 - 2 * core, members)).start()
-        own_last.start()
-        own.start()
-        start_far(1)
+                hop(n, chip, step, last(n)).start()
+
+        twin(n, chip, last(n), core).start()
+        own_last(n).start()
+        start_all(n)
+
+    gather(*cuts[0])
+    pl.semaphore_wait(barrier, members - 1)
+    launch(0)
+    gather(*cuts[1])
+    launch(1)
+    for n in range(2):
         for far in range(1, chips):
             for step in (1, -1):
                 origin = chip - step * far
 
                 @pl.when(has(-step * far))
                 def _():
-                    held = shelf(origin, core)
-                    hop(origin, step, held).wait_recv()
-                    twin(origin, held).start()
+                    held = shelf(n, origin, core)
+                    hop(n, origin, step, held).wait_recv()
+                    twin(n, origin, held, core).start()
 
                     @pl.when(has(step))
                     def _():
-                        hop(origin, step, held).start()
-
-            if far + 1 < chips:
-                start_far(far + 1)
-
-        own_last.wait()
-        twin(chip, send_ref.at[last]).wait_send()
-        twin(chip, shelf(chip, 1 - core)).wait_recv()
+                        hop(n, origin, step, held).start()
+
+    for n in range(2):
+        own_last(n).wait()
+        twin(n, chip, last(n), core).wait_send()
+        twin(n, chip, last(n), 1 - core).wait_recv()
         for step in (1, -1):
 
             @pl.when(has(step))
             def _():
-                hop(chip, step, send_ref.at[last]).wait_send()
+                hop(n, chip, step, last(n)).wait_send()
 
         for far in range(1, chips):
             for step in (1, -1):
@@ -134,46 +182,44 @@
 
                 @pl.when(has(-step * far))
                 def _():
-                    held = shelf(origin, core)
-                    twin(origin, held).wait_send()
-                    pltpu.make_async_remote_copy(
-                        src_ref=held,
-                        dst_ref=shelf(origin, 1 - core),
-                        send_sem=twin_send.at[origin],
-                        recv_sem=twin_recv.at[origin],
-                        device_id={"member": chip * 2 + 1 - core},
-                        device_id_type=MESH,
-                    ).wait_recv()
+                    held = shelf(n, origin, core)
+                    twin(n, origin, held, core).wait_send()
+                    twin(n, origin, held, 1 - core).wait_recv()
 
                     @pl.when(has(step))
                     def _():
-                        hop(origin, step, held).wait_send()
-
-    else:
-        lax.fori_loop(1, members, start, 0)
-        own.start()
-    own.wait()
-    lax.fori_loop(1, members, finish, 0)
-
-
-def exchange(send, members, slots, spill, total):
-    width = send.shape[1]
+                        hop(n, origin, step, held).wait_send()
+
+        finish_all(n)
+    blank.wait()
+
+
+def exchange(pick, a_rows, p_rows, members, slots, spill, total):
+    size, step_lanes = a_rows.shape[0], p_rows.shape[0]
     dma = pltpu.SemaphoreType.DMA
-    sems = [dma((members,)), dma((members,)), dma((2,))]
+    width = size + step_lanes
+    sems = [dma((2, members)), dma((2, members)), dma((2, 2))]
     if spill:
         chips = members // 2
-        sems += [dma((chips, 2)), dma((chips,)), dma((chips,)), dma((chips,))]
+        sems += [dma((2, chips, 2)), dma((2, chips)), dma((2, chips)), dma((2, chips))]
     return pl.pallas_call(
-        functools.partial(exchange_kernel, members, slots, spill),
-        out_shape=jax.ShapeDtypeStruct((total, width), send.dtype),
-        in_specs=[pl.BlockSpec(memory_space=pl.ANY)],
+        functools.partial(exchange_kernel, members, slots, spill, step_lanes),
+        out_shape=jax.ShapeDtypeStruct((total, width), a_rows.dtype),
+        in_specs=[pl.BlockSpec(memory_space=pltpu.VMEM)] * 3,
         out_specs=pl.BlockSpec(memory_space=pl.ANY),
-        scratch_shapes=sems,
+        scratch_shapes=[
+            pltpu.VMEM((pick.shape[0], width), a_rows.dtype),
+            pltpu.VMEM((16, width), a_rows.dtype),
+            dma,
+        ]
+        + sems,
         compiler_params=pltpu.CompilerParams(
-            collective_id=1 if spill else 0, has_side_effects=True
+            collective_id=1 if spill else 0,
+            has_side_effects=True,
+            vmem_limit_bytes=44 * 1024 * 1024,
         ),
         name="exchange_spill" if spill else "exchange_rows",
-    )(send)
+    )(pick, a_rows, p_rows)
 
 
 def counts_kernel(groups, members, own_ref, all_ref, send_sem, recv_sem):
@@ -395,27 +441,20 @@
         table = lax.all_gather(counts, "member")
     got = lax.dynamic_index_in_dim(table, me, 1, keepdims=False)
 
-    dense = jnp.concatenate(
-        [
-            a_band.transpose(1, 3, 2, 0).reshape(size, rows),
-            p_tent.transpose(1, 2, 0).reshape(modes * tile, rows),
-        ],
-        0,
-    )
+    a_rows = a_band.transpose(1, 3, 2, 0).reshape(size, rows)
+    p_rows = p_tent.transpose(1, 2, 0).reshape(modes * tile, rows)
     member = jnp.arange(members)
     upto = member[None, :] <= member[:, None]
     starts = jnp.sum(jnp.where(upto, got[None, :], 0), 1) - got
 
-    def sorted_send(flat_slot, count):
-        pick = (jnp.arange(count, dtype=i32)[:, None] == flat_slot[None, :]).astype(bf16)
-        return lax.dot_general(
-            pick, dense, (((1,), (1,)), ((), ())), preferred_element_type=jnp.float32
-        ).astype(bf16)
+    def picked(flat_slot, count):
+        return (jnp.arange(count, dtype=i32)[:, None] == flat_slot[None, :]).astype(bf16)
 
     flat_slot = new_owner * slots + place
 
-    def direct(send):
-        return exchange(send, members, slots, 0, total + 16)
+    def direct(own_a, own_p):
+        pick = picked(flat_slot, members * slots)
+        return exchange(pick, own_a, own_p, members, slots, 0, total + 16)
 
     def direct_lands():
         within = jnp.arange(slots, dtype=i32)
@@ -433,8 +472,9 @@
             place < few, new_owner * few + place, members * few + base + place - few
         )
 
-        def spilled(send):
-            return exchange(send, members, few, spill, total + 16)
+        def spilled(own_a, own_p):
+            pick = picked(spill_slot, members * few + spill)
+            return exchange(pick, own_a, own_p, members, few, spill, total + 16)
 
         def spilled_lands():
             within = jnp.arange(few, dtype=i32)
@@ -450,16 +490,16 @@
             return jnp.pad(lands, (0, total - members * (few + spill)), constant_values=-width)
 
         lands = jnp.where(fits, spilled_lands(), direct_lands())
-        send = sorted_send(jnp.where(fits, spill_slot, flat_slot), members * slots)
-        recv = lax.cond(fits, spilled, direct, send)
+        recv = lax.cond(fits, spilled, direct, a_rows, p_rows)
     else:
         lands = direct_lands()
-        recv = direct(sorted_send(flat_slot, members * slots))
+        recv = direct(a_rows, p_rows)
 
     edge = jnp.arange(16, dtype=i32)
     edge_row = jnp.where(edge < HALO, edge, jnp.where(edge < 2 * HALO, rows - 2 * HALO + edge, -1))
-    rim_pick = (edge_row[:, None] == lands[None, :]).astype(bf16)
-    rim = jnp.dot(rim_pick, recv[:total], preferred_element_type=jnp.float32).astype(bf16)
+    filled = jnp.concatenate([lands, jnp.full((16,), -width, i32)])
+    rim_pick = (edge_row[:, None] == filled[None, :]).astype(bf16)
+    rim = jnp.dot(rim_pick, recv, preferred_element_type=jnp.float32).astype(bf16)
     devices = groups * members
     up = [(i, i + 1) for i in range(devices - 1)]
     down = [(i + 1, i) for i in range(devices - 1)]

time: 276 us -> 272 us (0.986)
  matrix products: 19.7 us -> 10.6 us
  Pallas kernels: 219 us -> 224 us
    dot_general x2 -> x1, matrix products: 14.6 us -> 5.51 us  [per_device(): jnp.dot(rim_pick, recv, preferred_element_type=jnp.float32).astype(bf16)]
    pallas_call x1, Pallas kernels: 172 us -> 176 us  [exchange(): pl.pallas_call(functools.partial(exchange_kernel, members, slots, spill,...]
where the time goes in v4:
time: 272 us
  Pallas kernels  224 us (82%)
  local copies, waits for them, and re-layouts  15.3 us (6%)
  matrix products  10.6 us (4%)
  waiting for transfers between devices  7.33 us (3%)
  starting transfers between devices  6.82 us (3%)
  other arithmetic  6.36 us (2%)
    pallas_call x1, Pallas kernels, exchange(): pl.pallas_call(functools.partial(exchange_kernel, members, slots, spill,...  176 us
    pallas_call x1, Pallas kernels, setup(): pl.pallas_call(setup_kernel, out_shape=(jax.ShapeDtypeStruct((3, modes, t...  38.3 us
    pallas_call x1, Pallas kernels, share_counts(): pl.pallas_call(functools.partial(counts_kernel, groups, members), out_sha...  9.25 us
    transpose x1, local copies, waits for them, and re-layouts, per_device(): a_rows = a_band.transpose(1, 3, 2, 0).reshape(size, rows)  9 us
    ppermute x1, waiting for transfers between devices, per_device(): from_right = lax.ppermute(rim[:HALO], axes, down)  7.33 us
    dot_general x1, matrix products, per_device(): jnp.dot(rim_pick, recv, preferred_element_type=jnp.float32).astype(bf16)  5.51 us
  transfers between devices with their start and end apart: 2, of which 1 were waited for; matrix products, arithmetic and copies ran while one was open for 0% of the time, Pallas kernels for 0%

profile of v4, /device:TPU:27, one launch (start us, length us, event | category | flops | bytes accessed | tf_op | source)
XLA Modules:
  0.0 271.7 jit_solution(18158432188391908209)
XLA Ops:
  0.6 0.0 copy-start.3
  0.6 0.0 copy-start.2
  0.7 0.9 convert_reduce_fusion.1
  1.5 0.5 pad_bitcast_fusion.own_ref
  2.0 9.2 %share_counts.1 = s32[32,1,128]{2,1,0:T(1,128)} custom-call(s32[1,128]{1,0:T(1,128)} %pad_bitcast_fusion.own_ref), custom_call_target="tpu_custom_call" | custom-call | tf_op jit(solution)/shard_map/share_counts/pallas_call | solution.py:267
  11.3 1.4 fusion.17
  12.7 0.3 dynamic-slice_reduce_fusion
  13.0 0.1 select_reduce_fusion.3
  13.2 0.1 add_select_fusion
  13.2 0.1 add_select_fusion.2
  13.3 0.9 fusion.4
  14.2 0.7 iota_compare_fusion.7
  14.9 0.1 select_reduce_fusion.2
  15.1 0.1 add_select_fusion.1
  15.1 0.1 select_n.96
  15.2 0.1 select_n.98
  15.3 0.1 select_n.93
  15.4 9.0 %copy.7 = bf16[3,64,64,192]{3,2,1,0:T(8,128)(2,1)} copy(bf16[3,64,64,192]{3,1,2,0:T(8,128)(2,1)} %bitcast.17) | data formatting | bytes 9437184 | tf_op jit(solution)/shard_map/transpose | solution.py:444
  24.4 0.6 reduce_max.9
  25.7 0.0 copy-done.3
  25.7 0.0 copy-done.2
  25.7 176.5 %conditional.1 = (bf16[400,12672]{1,0:T(8,128)(2,1)}) conditional(s32[]{:T(128)} %convert_element_type.38, (s32[192]{0:T(256)S(1)}, s32[192]{0:T(256)S(1)}, bf16[12288,192]{1,0:T(8,128)(2,1)}, bf16[384,192]{1,0:T(8,128)(2,1)S(1)}) %tuple.51, (s32[192]{0:T(256)S(1)}, s32[192]{0:T(256)S(1)}, s32[8]{0:T(128)S(1)}, pred[8,8]{1,0:T(8,128)(4,1)S(1)}, ...), branch_computations={%region_4.5_spmd, %region_5.8_spmd} | conditional | flops 147840 | bytes 150536 | solution.py:493
  25.8 0.1 select_reduce_fusion.1
  25.9 0.1 select_reduce_fusion
  26.0 176.2 %exchange_spill.2 = bf16[400,12672]{1,0:T(8,128)(2,1)} custom-call(bf16[272,192]{1,0:T(8,128)(2,1)S(1)} %fusion.1.pick_ref, bf16[12288,192]{1,0:T(8,128)(2,1)} %get-tuple-element.129.a_ref, bf16[384,192]{1,0:T(8,128)(2,1)S(1)} %get-tuple-element.130.p_ref), custom_call_target="tpu_custom_call" | custom-call | tf_op jit(solution)/shard_map/cond/branch_1_fun/exchange_spill/pallas_call | solution.py:205
  202.3 0.0 copy-start
  202.3 5.5 %convolution_convert_fusion.1 = bf16[16,12672]{1,0:T(8,128)(2,1)S(1)} fusion(bf16[400,12672]{1,0:T(8,128)(2,1)} %get-tuple-element.148, s32[400]{0:T(512)S(1)} %concatenate.13, s32[16]{0:T(128)S(1)} %compare_select_fusion.2), kind=kOutput, calls=%fused_computation.11 | convolution fusion | flops 162410752 | bytes 10544768 | tf_op jit(solution)/shard_map/dot_general | solution.py:502
  207.8 0.1 fusion.16
  207.9 4.7 %collective-permute-start = (bf16[3,12672]{1,0:T(4,128)(2,1)S(1)}, bf16[3,12672]{1,0:T(4,128)(2,1)S(1)}, u32[]{:S(2)}, u32[]{:S(2)}) collective-permute-start(bf16[3,12672]{1,0:T(4,128)(2,1)S(1)} %get-tuple-element.143), channel_id=1, source_target_pairs={{0,1},{1,2},{2,3},{3,4},{4,5},{5,6},{6,7},{7,8},{8,9},{9,10},{10,1... | collective-permute-start | bytes 228104 | tf_op jit(solution)/shard_map/ppermute | solution.py:506
  212.6 2.1 collective-permute-start.1
  214.8 0.1 pad.10.clone
  214.8 0.0 collective-permute-done
  214.9 7.3 %collective-permute-done.1 = bf16[3,12672]{1,0:T(4,128)(2,1)S(1)} collective-permute-done((bf16[3,12672]{1,0:T(4,128)(2,1)S(1)}, bf16[3,12672]{1,0:T(4,128)(2,1)S(1)}, u32[]{:S(2)}, u32[]{:S(2)}) %collective-permute-start.1) | collective-permute-done | bytes 76064 | tf_op jit(solution)/shard_map/ppermute | solution.py:507
  222.2 0.0 copy-done
  222.2 0.2 maximum_dynamic-update-slice_fusion
  222.4 4.2 %convolution_convert_fusion.ext_ref = bf16[12672,256]{1,0:T(8,128)(2,1)S(1)} fusion(bf16[400,12672]{1,0:T(8,128)(2,1)S(1)} %maximum_dynamic-update-slice_fusion, s32[400]{0:T(512)S(1)} %pad_add_fusion), kind=kOutput, calls=%fused_computation.10 | convolution fusion | flops 2598572032 | bytes 16627264 | tf_op jit(solution)/shard_map/dot_general | solution.py:515
  226.5 0.0 copy-start.1
  226.5 0.1 slice.26
  226.7 1.8 convert_reduce_fusion.dg_ref
  228.5 0.8 copy-done.1
  229.3 38.3 %coarse_setup.1 = (bf16[3,6,64,256]{3,2,1,0:T(8,128)(2,1)}, f32[7,6,6,256]{3,2,1,0:T(8,128)}) custom-call(bf16[12672,256]{1,0:T(8,128)(2,1)} %copy-done.1, f32[64,256]{1,0:T(8,128)} %convert_reduce_fusion.dg_ref), custom_call_target="tpu_custom_call" | custom-call | tf_op jit(solution)/shard_map/coarse_setup/pallas_call | solution.py:397
  267.6 1.1 slice.23
  268.7 0.8 copy.8
  269.5 2.1 slice_bitcast_fusion
  (18 shorter events, 0.2 us)
Async XLA Ops:
  0.6 25.1 %copy-start.3 = (s32[192]{0:T(256)S(1)}, s32[192]{0:T(256)}, u32[]{:S(2)}) copy-start(s32[192]{0:T(256)} %param.7) | copy-start | bytes 2308
  0.6 25.1 %copy-start.2 = (bf16[192,6,64]{0,2,1:T(8,128)(2,1)S(1)}, bf16[192,6,64]{0,2,1:T(8,128)(2,1)}, u32[]{:S(2)}) copy-start(bf16[192,6,64]{0,2,1:T(8,128)(2,1)} %param.6) | copy-start | bytes 442372
  202.3 19.9 %copy-start = (bf16[400,12672]{1,0:T(8,128)(2,1)S(1)}, bf16[400,12672]{1,0:T(8,128)(2,1)}, u32[]{:S(2)}) copy-start(bf16[400,12672]{1,0:T(8,128)(2,1)} %get-tuple-element.148) | copy-start | bytes 30412804
  207.9 7.0 %collective-permute-start = (bf16[3,12672]{1,0:T(4,128)(2,1)S(1)}, bf16[3,12672]{1,0:T(4,128)(2,1)S(1)}, u32[]{:S(2)}, u32[]{:S(2)}) collective-permute-start(bf16[3,12672]{1,0:T(4,128)(2,1)S(1)} %get-tuple-element.143), channel_id=1, source_target_pairs={{0,1},{1,2},{2,3},{3,4},{4,5},{5,6},{6,7},{7,8},{8,9},{9,10},{10,1... | collective-permute-start | bytes 228104 | tf_op jit(solution)/shard_map/ppermute | solution.py:506
  212.6 9.6 %collective-permute-start.1 = (bf16[3,12672]{1,0:T(4,128)(2,1)S(1)}, bf16[3,12672]{1,0:T(4,128)(2,1)S(1)}, u32[]{:S(2)}, u32[]{:S(2)}) collective-permute-start(bf16[3,12672]{1,0:T(4,128)(2,1)S(1)} %get-tuple-element.144), channel_id=1, source_target_pairs={{1,0},{2,1},{3,2},{4,3},{5,4},{6,5},{7,6},{8,7},{9,8},{10,9},{11,1... | collective-permute-start | bytes 228104 | tf_op jit(solution)/shard_map/ppermute | solution.py:507
  226.5 2.8 %copy-start.1 = (bf16[12672,256]{1,0:T(8,128)(2,1)}, bf16[12672,256]{1,0:T(8,128)(2,1)S(1)}, u32[]{:S(2)}) copy-start(bf16[12672,256]{1,0:T(8,128)(2,1)S(1)} %convolution_convert_fusion.ext_ref) | copy-start | bytes 19464196

commit v5 on v4

--- a/solution.py
+++ b/solution.py
@@ -284,12 +284,19 @@
     return x
 
 
-def setup_kernel(ext_ref, dg_ref, s_ref, co_ref, p3, s3, ap3, dinv):
-    _, modes, tile, width = s_ref.shape
+def setup_kernel(ext_ref, s_ref, co_ref, p3, s3, ap3, dinv, tiles, wide):
+    _, modes, tile, rows = s_ref.shape
+    width = ext_ref.shape[1]
     f32 = jnp.float32
     half = tile // 2
     parts = [(i, l) for l in range(width // LANES) for i in range(2)]
-    diag = dg_ref[...]
+    line = lax.broadcasted_iota(jnp.int32, (tile, width), 0)
+
+    def pick_diag(j, total):
+        at = pl.multiple_of((tile + j) * tile, tile)
+        return total + jnp.where(line == j, ext_ref[pl.ds(at, tile), :].astype(f32), 0.0)
+
+    diag = lax.fori_loop(0, tile, pick_diag, jnp.zeros((tile, width), f32))
     dinv[...] = jnp.where(diag > 1.0, 1.0 / jnp.where(diag > 1.0, diag, 1.0), 0.0)
     for c in range(modes):
         own = ext_ref[pl.ds((3 * tile + c) * tile, tile), :].astype(f32)
@@ -334,7 +341,6 @@
                 if k == 1:
                     value = p3[1, c, pl.ds(i0, half), pl.ds(l0, LANES)] + value
                 value = value.astype(jnp.bfloat16)
-                s_ref[k, c, pl.ds(i0, half), pl.ds(l0, LANES)] = value
                 s3[1, k, c, pl.ds(i0, half), pl.ds(l0, LANES)] = value.astype(f32)
 
         each_part(smooth)
@@ -342,6 +348,7 @@
     def spread_s(q, carry):
         t, c = q // modes, q % modes
         own = s3[1, t, c]
+        s_ref[t, c] = pltpu.roll(own, width - HALO, axis=1)[:, :rows].astype(jnp.bfloat16)
         s3[0, t, c] = shifted(own, 0)
         s3[2, t, c] = shifted(own, 2)
         return carry
@@ -385,32 +392,43 @@
                     term = jnp.sum(term.reshape(tile // 8, 8, LANES), axis=0)
                     sums[d] = term if sums[d] is None else sums[d] + term
             for d in range(modes):
-                co_ref[f, c, d : d + 1, lanes] = jnp.sum(sums[d], axis=0, keepdims=True)
+                tiles[f, c, d : d + 1, lanes] = jnp.sum(sums[d], axis=0, keepdims=True)
             return carry
 
         lax.fori_loop(0, modes * (width // LANES), coarse, 0)
 
-
-def setup(ext, diag, modes, tile):
+    count = 7 * modes * modes
+    for f in range(7):
+        for c in range(modes):
+            at = (f * modes + c) * modes
+            wide[at : at + modes, :] = tiles[f, c]
+    wide[count:] = jnp.zeros((wide.shape[0] - count, width), f32)
+    co_ref[...] = jnp.transpose(pltpu.roll(wide[...], width - HALO, axis=1))[:rows, :count]
+
+
+def setup(ext, modes, tile, rows):
     width = ext.shape[1]
+    count = 7 * modes * modes
     f32 = jnp.float32
     return pl.pallas_call(
         setup_kernel,
         out_shape=(
-            jax.ShapeDtypeStruct((3, modes, tile, width), jnp.bfloat16),
-            jax.ShapeDtypeStruct((7, modes, modes, width), f32),
+            jax.ShapeDtypeStruct((3, modes, tile, rows), jnp.bfloat16),
+            jax.ShapeDtypeStruct((rows, count), f32),
         ),
-        in_specs=[pl.BlockSpec(memory_space=pltpu.VMEM)] * 2,
+        in_specs=[pl.BlockSpec(memory_space=pltpu.VMEM)],
         out_specs=(pl.BlockSpec(memory_space=pltpu.VMEM),) * 2,
         scratch_shapes=[
             pltpu.VMEM((3, modes, tile, width), f32),
             pltpu.VMEM((3, 3, modes, tile, width), f32),
             pltpu.VMEM((3, 5, modes, tile, width), f32),
             pltpu.VMEM((tile, width), f32),
+            pltpu.VMEM((7, modes, modes, width), f32),
+            pltpu.VMEM((-(-count // LANES) * LANES, width), f32),
         ],
-        compiler_params=pltpu.CompilerParams(vmem_limit_bytes=56 * 1024 * 1024),
+        compiler_params=pltpu.CompilerParams(vmem_limit_bytes=28 * 1024 * 1024),
         name="coarse_setup",
-    )(ext, diag)
+    )(ext)
 
 
 def per_device(a_band, p_tent, new_owner):
@@ -515,13 +533,8 @@
     ext = lax.dot_general(
         recv, place_out, (((0,), (0,)), ((), ())), preferred_element_type=jnp.float32
     ).astype(bf16)
-    centre = ext[tile * tile : 2 * tile * tile].reshape(tile, tile, width)
-    eye = jnp.eye(tile, dtype=bf16)[:, :, None]
-    diag = jnp.sum((centre * eye).astype(jnp.float32), 0)
-    s_out, co = setup(ext, diag, modes, tile)
-    p_smooth = s_out[..., HALO : HALO + rows].transpose(3, 0, 1, 2)
-    coarse = co[..., HALO : HALO + rows].reshape(7 * modes * modes, rows).T
-    return (p_smooth, coarse)
+    s_out, coarse = setup(ext, modes, tile, rows)
+    return (s_out.transpose(3, 0, 1, 2), coarse)
 
 
 def solution(mesh):

time: 272 us -> 263 us (0.967)
  local copies, waits for them, and re-layouts: 15.3 us -> 10.2 us
where the time goes in v5:
time: 263 us
  Pallas kernels  222 us (84%)
  matrix products  10.6 us (4%)
  local copies, waits for them, and re-layouts  10.2 us (4%)
  waiting for transfers between devices  7.35 us (3%)
  starting transfers between devices  6.82 us (3%)
  other arithmetic  4.52 us (2%)
    pallas_call x1, Pallas kernels, exchange(): pl.pallas_call(functools.partial(exchange_kernel, members, slots, spill,...  176 us
    pallas_call x1, Pallas kernels, setup(): pl.pallas_call(setup_kernel, out_shape=(jax.ShapeDtypeStruct((3, modes, t...  36.5 us
    pallas_call x1, Pallas kernels, share_counts(): pl.pallas_call(functools.partial(counts_kernel, groups, members), out_sha...  9.25 us
    transpose x1, local copies, waits for them, and re-layouts, per_device(): a_rows = a_band.transpose(1, 3, 2, 0).reshape(size, rows)  9 us
    ppermute x1, waiting for transfers between devices, per_device(): from_right = lax.ppermute(rim[:HALO], axes, down)  7.34 us
    dot_general x1, matrix products, per_device(): jnp.dot(rim_pick, recv, preferred_element_type=jnp.float32).astype(bf16)  5.51 us
  transfers between devices with their start and end apart: 2, of which 1 were waited for; matrix products, arithmetic and copies ran while one was open for 0% of the time, Pallas kernels for 0%

profile of v5, /device:TPU:27, one launch (start us, length us, event | category | flops | bytes accessed | tf_op | source)
XLA Modules:
  0.0 263.0 jit_solution(7212917491432169799)
XLA Ops:
  0.6 0.0 copy-start.2
  0.6 0.0 copy-start.1
  0.7 0.9 convert_reduce_fusion
  1.5 0.5 pad_bitcast_fusion.own_ref
  2.0 9.2 %share_counts.1 = s32[32,1,128]{2,1,0:T(1,128)} custom-call(s32[1,128]{1,0:T(1,128)} %pad_bitcast_fusion.own_ref), custom_call_target="tpu_custom_call" | custom-call | tf_op jit(solution)/shard_map/share_counts/pallas_call | solution.py:267
  11.3 1.4 fusion.16
  12.7 0.3 dynamic-slice_reduce_fusion
  13.0 0.1 select_reduce_fusion.3
  13.2 0.1 add_select_fusion
  13.2 0.1 add_select_fusion.2
  13.3 0.9 fusion.4
  14.2 0.7 iota_compare_fusion.6
  14.9 0.1 select_reduce_fusion.2
  15.1 0.1 add_select_fusion.1
  15.1 0.1 select_n.96
  15.2 0.1 select_n.98
  15.3 0.1 select_n.93
  15.4 9.0 %copy.6 = bf16[3,64,64,192]{3,2,1,0:T(8,128)(2,1)} copy(bf16[3,64,64,192]{3,1,2,0:T(8,128)(2,1)} %bitcast.13) | data formatting | bytes 9437184 | tf_op jit(solution)/shard_map/transpose | solution.py:462
  24.4 0.6 reduce_max.9
  25.7 0.0 copy-done.2
  25.7 0.0 copy-done.1
  25.7 176.5 %conditional.1 = (bf16[400,12672]{1,0:T(8,128)(2,1)}) conditional(s32[]{:T(128)} %convert_element_type.28, (s32[192]{0:T(256)S(1)}, s32[192]{0:T(256)S(1)}, bf16[12288,192]{1,0:T(8,128)(2,1)}, bf16[384,192]{1,0:T(8,128)(2,1)S(1)}) %tuple.50, (s32[192]{0:T(256)S(1)}, s32[192]{0:T(256)S(1)}, s32[8]{0:T(128)S(1)}, pred[8,8]{1,0:T(8,128)(4,1)S(1)}, ...), branch_computations={%region_4.5_spmd, %region_5.8_spmd} | conditional | flops 147840 | bytes 150536 | solution.py:511
  25.8 0.1 select_reduce_fusion.1
  25.9 0.1 select_reduce_fusion
  26.0 176.2 %exchange_spill.2 = bf16[400,12672]{1,0:T(8,128)(2,1)} custom-call(bf16[272,192]{1,0:T(8,128)(2,1)S(1)} %fusion.1.pick_ref, bf16[12288,192]{1,0:T(8,128)(2,1)} %get-tuple-element.129.a_ref, bf16[384,192]{1,0:T(8,128)(2,1)S(1)} %get-tuple-element.130.p_ref), custom_call_target="tpu_custom_call" | custom-call | tf_op jit(solution)/shard_map/cond/branch_1_fun/exchange_spill/pallas_call | solution.py:205
  202.3 0.0 copy-start
  202.3 5.5 %convolution_convert_fusion.1 = bf16[16,12672]{1,0:T(8,128)(2,1)S(1)} fusion(bf16[400,12672]{1,0:T(8,128)(2,1)} %get-tuple-element.146, s32[400]{0:T(512)S(1)} %concatenate.13, s32[16]{0:T(128)S(1)} %compare_select_fusion.2), kind=kOutput, calls=%fused_computation.11 | convolution fusion | flops 162410752 | bytes 10544768 | tf_op jit(solution)/shard_map/dot_general | solution.py:520
  207.8 0.1 fusion.15
  207.9 4.7 %collective-permute-start = (bf16[3,12672]{1,0:T(4,128)(2,1)S(1)}, bf16[3,12672]{1,0:T(4,128)(2,1)S(1)}, u32[]{:S(2)}, u32[]{:S(2)}) collective-permute-start(bf16[3,12672]{1,0:T(4,128)(2,1)S(1)} %get-tuple-element.141), channel_id=1, source_target_pairs={{0,1},{1,2},{2,3},{3,4},{4,5},{5,6},{6,7},{7,8},{8,9},{9,10},{10,1... | collective-permute-start | bytes 228104 | tf_op jit(solution)/shard_map/ppermute | solution.py:524
  212.6 2.1 collective-permute-start.1
  214.7 0.1 pad.10.clone
  214.8 0.0 collective-permute-done
  214.8 7.3 %collective-permute-done.1 = bf16[3,12672]{1,0:T(4,128)(2,1)S(1)} collective-permute-done((bf16[3,12672]{1,0:T(4,128)(2,1)S(1)}, bf16[3,12672]{1,0:T(4,128)(2,1)S(1)}, u32[]{:S(2)}, u32[]{:S(2)}) %collective-permute-start.1) | collective-permute-done | bytes 76064 | tf_op jit(solution)/shard_map/ppermute | solution.py:525
  222.2 0.0 copy-done
  222.2 0.2 maximum_dynamic-update-slice_fusion
  222.4 4.2 %convolution_convert_fusion.ext_ref = bf16[12672,256]{1,0:T(8,128)(2,1)S(1)} fusion(bf16[400,12672]{1,0:T(8,128)(2,1)S(1)} %maximum_dynamic-update-slice_fusion, s32[400]{0:T(512)S(1)} %pad_add_fusion), kind=kOutput, calls=%fused_computation.10 | convolution fusion | flops 2598572032 | bytes 16627264 | tf_op jit(solution)/shard_map/dot_general | solution.py:533
  226.5 36.5 %coarse_setup.1 = (bf16[3,6,64,192]{3,2,1,0:T(8,128)(2,1)}, f32[192,252]{1,0:T(8,128)}) custom-call(bf16[12672,256]{1,0:T(8,128)(2,1)S(1)} %convolution_convert_fusion.ext_ref), custom_call_target="tpu_custom_call" | custom-call | tf_op jit(solution)/shard_map/coarse_setup/pallas_call | solution.py:413
  (16 shorter events, 0.1 us)
Async XLA Ops:
  0.6 25.1 %copy-start.2 = (s32[192]{0:T(256)S(1)}, s32[192]{0:T(256)}, u32[]{:S(2)}) copy-start(s32[192]{0:T(256)} %param.7) | copy-start | bytes 2308
  0.6 25.1 %copy-start.1 = (bf16[192,6,64]{0,2,1:T(8,128)(2,1)S(1)}, bf16[192,6,64]{0,2,1:T(8,128)(2,1)}, u32[]{:S(2)}) copy-start(bf16[192,6,64]{0,2,1:T(8,128)(2,1)} %param.6) | copy-start | bytes 442372
  202.3 19.9 %copy-start = (bf16[400,12672]{1,0:T(8,128)(2,1)S(1)}, bf16[400,12672]{1,0:T(8,128)(2,1)}, u32[]{:S(2)}) copy-start(bf16[400,12672]{1,0:T(8,128)(2,1)} %get-tuple-element.146) | copy-start | bytes 30412804
  207.9 6.9 %collective-permute-start = (bf16[3,12672]{1,0:T(4,128)(2,1)S(1)}, bf16[3,12672]{1,0:T(4,128)(2,1)S(1)}, u32[]{:S(2)}, u32[]{:S(2)}) collective-permute-start(bf16[3,12672]{1,0:T(4,128)(2,1)S(1)} %get-tuple-element.141), channel_id=1, source_target_pairs={{0,1},{1,2},{2,3},{3,4},{4,5},{5,6},{6,7},{7,8},{8,9},{9,10},{10,1... | collective-permute-start | bytes 228104 | tf_op jit(solution)/shard_map/ppermute | solution.py:524
  212.6 9.6 %collective-permute-start.1 = (bf16[3,12672]{1,0:T(4,128)(2,1)S(1)}, bf16[3,12672]{1,0:T(4,128)(2,1)S(1)}, u32[]{:S(2)}, u32[]{:S(2)}) collective-permute-start(bf16[3,12672]{1,0:T(4,128)(2,1)S(1)} %get-tuple-element.142), channel_id=1, source_target_pairs={{1,0},{2,1},{3,2},{4,3},{5,4},{6,5},{7,6},{8,7},{9,8},{10,9},{11,1... | collective-permute-start | bytes 228104 | tf_op jit(solution)/shard_map/ppermute | solution.py:525

commit v6 on v5

--- a/solution.py
+++ b/solution.py
@@ -72,11 +72,12 @@
         )
 
     def start_all(n):
-        def start(o, carry):
-            copy(n, o).start()
+        def start(i, carry):
+            far = members // 2 + jnp.where(i % 2 == 1, (i + 1) // 2, -(i // 2))
+            copy(n, far).start()
             return carry
 
-        lax.fori_loop(1, members, start, 0)
+        lax.fori_loop(0, members - 1, start, 0)
         own(n).start()
 
     def finish_all(n):

time: 263 us -> 263 us (level)
  no operation moved by 1% of the time
where the time goes in v6:
time: 263 us
  Pallas kernels  222 us (84%)
  matrix products  10.6 us (4%)
  local copies, waits for them, and re-layouts  10.2 us (4%)
  waiting for transfers between devices  7.35 us (3%)
  starting transfers between devices  6.82 us (3%)
  other arithmetic  4.52 us (2%)
    pallas_call x1, Pallas kernels, exchange(): pl.pallas_call(functools.partial(exchange_kernel, members, slots, spill,...  176 us
    pallas_call x1, Pallas kernels, setup(): pl.pallas_call(setup_kernel, out_shape=(jax.ShapeDtypeStruct((3, modes, t...  36.5 us
    pallas_call x1, Pallas kernels, share_counts(): pl.pallas_call(functools.partial(counts_kernel, groups, members), out_sha...  9.25 us
    transpose x1, local copies, waits for them, and re-layouts, per_device(): a_rows = a_band.transpose(1, 3, 2, 0).reshape(size, rows)  9 us
    ppermute x1, waiting for transfers between devices, per_device(): from_right = lax.ppermute(rim[:HALO], axes, down)  7.34 us
    dot_general x1, matrix products, per_device(): jnp.dot(rim_pick, recv, preferred_element_type=jnp.float32).astype(bf16)  5.51 us
  transfers between devices with their start and end apart: 2, of which 1 were waited for; matrix products, arithmetic and copies ran while one was open for 0% of the time, Pallas kernels for 0%

profile of v6, /device:TPU:27, one launch (start us, length us, event | category | flops | bytes accessed | tf_op | source)
XLA Modules:
  0.0 263.0 jit_solution(7736789841326066701)
XLA Ops:
  0.6 0.0 copy-start.2
  0.6 0.0 copy-start.1
  0.7 0.9 convert_reduce_fusion
  1.5 0.5 pad_bitcast_fusion.own_ref
  2.0 9.2 %share_counts.1 = s32[32,1,128]{2,1,0:T(1,128)} custom-call(s32[1,128]{1,0:T(1,128)} %pad_bitcast_fusion.own_ref), custom_call_target="tpu_custom_call" | custom-call | tf_op jit(solution)/shard_map/share_counts/pallas_call | solution.py:268
  11.3 1.4 fusion.16
  12.7 0.3 dynamic-slice_reduce_fusion
  13.0 0.1 select_reduce_fusion.3
  13.2 0.1 add_select_fusion
  13.2 0.1 add_select_fusion.2
  13.3 0.9 fusion.4
  14.2 0.7 iota_compare_fusion.6
  14.9 0.1 select_reduce_fusion.2
  15.1 0.1 add_select_fusion.1
  15.1 0.1 select_n.96
  15.2 0.1 select_n.98
  15.3 0.1 select_n.93
  15.4 9.0 %copy.6 = bf16[3,64,64,192]{3,2,1,0:T(8,128)(2,1)} copy(bf16[3,64,64,192]{3,1,2,0:T(8,128)(2,1)} %bitcast.13) | data formatting | bytes 9437184 | tf_op jit(solution)/shard_map/transpose | solution.py:463
  24.4 0.6 reduce_max.9
  25.7 0.0 copy-done.2
  25.7 0.0 copy-done.1
  25.7 176.5 %conditional.1 = (bf16[400,12672]{1,0:T(8,128)(2,1)}) conditional(s32[]{:T(128)} %convert_element_type.28, (s32[192]{0:T(256)S(1)}, s32[192]{0:T(256)S(1)}, bf16[12288,192]{1,0:T(8,128)(2,1)}, bf16[384,192]{1,0:T(8,128)(2,1)S(1)}) %tuple.50, (s32[192]{0:T(256)S(1)}, s32[192]{0:T(256)S(1)}, s32[8]{0:T(128)S(1)}, pred[8,8]{1,0:T(8,128)(4,1)S(1)}, ...), branch_computations={%region_4.5_spmd, %region_5.8_spmd} | conditional | flops 147840 | bytes 150536 | solution.py:512
  25.8 0.1 select_reduce_fusion.1
  25.9 0.1 select_reduce_fusion
  26.0 176.2 %exchange_spill.2 = bf16[400,12672]{1,0:T(8,128)(2,1)} custom-call(bf16[272,192]{1,0:T(8,128)(2,1)S(1)} %fusion.1.pick_ref, bf16[12288,192]{1,0:T(8,128)(2,1)} %get-tuple-element.129.a_ref, bf16[384,192]{1,0:T(8,128)(2,1)S(1)} %get-tuple-element.130.p_ref), custom_call_target="tpu_custom_call" | custom-call | tf_op jit(solution)/shard_map/cond/branch_1_fun/exchange_spill/pallas_call | solution.py:206
  202.3 0.0 copy-start
  202.3 5.5 %convolution_convert_fusion.1 = bf16[16,12672]{1,0:T(8,128)(2,1)S(1)} fusion(bf16[400,12672]{1,0:T(8,128)(2,1)} %get-tuple-element.146, s32[400]{0:T(512)S(1)} %concatenate.13, s32[16]{0:T(128)S(1)} %compare_select_fusion.2), kind=kOutput, calls=%fused_computation.11 | convolution fusion | flops 162410752 | bytes 10544768 | tf_op jit(solution)/shard_map/dot_general | solution.py:521
  207.8 0.1 fusion.15
  207.9 4.7 %collective-permute-start = (bf16[3,12672]{1,0:T(4,128)(2,1)S(1)}, bf16[3,12672]{1,0:T(4,128)(2,1)S(1)}, u32[]{:S(2)}, u32[]{:S(2)}) collective-permute-start(bf16[3,12672]{1,0:T(4,128)(2,1)S(1)} %get-tuple-element.141), channel_id=1, source_target_pairs={{0,1},{1,2},{2,3},{3,4},{4,5},{5,6},{6,7},{7,8},{8,9},{9,10},{10,1... | collective-permute-start | bytes 228104 | tf_op jit(solution)/shard_map/ppermute | solution.py:525
  212.6 2.1 collective-permute-start.1
  214.7 0.1 pad.10.clone
  214.8 0.0 collective-permute-done
  214.8 7.3 %collective-permute-done.1 = bf16[3,12672]{1,0:T(4,128)(2,1)S(1)} collective-permute-done((bf16[3,12672]{1,0:T(4,128)(2,1)S(1)}, bf16[3,12672]{1,0:T(4,128)(2,1)S(1)}, u32[]{:S(2)}, u32[]{:S(2)}) %collective-permute-start.1) | collective-permute-done | bytes 76064 | tf_op jit(solution)/shard_map/ppermute | solution.py:526
  222.2 0.0 copy-done
  222.2 0.2 maximum_dynamic-update-slice_fusion
  222.4 4.2 %convolution_convert_fusion.ext_ref = bf16[12672,256]{1,0:T(8,128)(2,1)S(1)} fusion(bf16[400,12672]{1,0:T(8,128)(2,1)S(1)} %maximum_dynamic-update-slice_fusion, s32[400]{0:T(512)S(1)} %pad_add_fusion), kind=kOutput, calls=%fused_computation.10 | convolution fusion | flops 2598572032 | bytes 16627264 | tf_op jit(solution)/shard_map/dot_general | solution.py:534
  226.5 36.5 %coarse_setup.1 = (bf16[3,6,64,192]{3,2,1,0:T(8,128)(2,1)}, f32[192,252]{1,0:T(8,128)}) custom-call(bf16[12672,256]{1,0:T(8,128)(2,1)S(1)} %convolution_convert_fusion.ext_ref), custom_call_target="tpu_custom_call" | custom-call | tf_op jit(solution)/shard_map/coarse_setup/pallas_call | solution.py:414
  (16 shorter events, 0.1 us)
Async XLA Ops:
  0.6 25.1 %copy-start.2 = (s32[192]{0:T(256)S(1)}, s32[192]{0:T(256)}, u32[]{:S(2)}) copy-start(s32[192]{0:T(256)} %param.7) | copy-start | bytes 2308
  0.6 25.1 %copy-start.1 = (bf16[192,6,64]{0,2,1:T(8,128)(2,1)S(1)}, bf16[192,6,64]{0,2,1:T(8,128)(2,1)}, u32[]{:S(2)}) copy-start(bf16[192,6,64]{0,2,1:T(8,128)(2,1)} %param.6) | copy-start | bytes 442372
  202.3 19.9 %copy-start = (bf16[400,12672]{1,0:T(8,128)(2,1)S(1)}, bf16[400,12672]{1,0:T(8,128)(2,1)}, u32[]{:S(2)}) copy-start(bf16[400,12672]{1,0:T(8,128)(2,1)} %get-tuple-element.146) | copy-start | bytes 30412804
  207.9 6.9 %collective-permute-start = (bf16[3,12672]{1,0:T(4,128)(2,1)S(1)}, bf16[3,12672]{1,0:T(4,128)(2,1)S(1)}, u32[]{:S(2)}, u32[]{:S(2)}) collective-permute-start(bf16[3,12672]{1,0:T(4,128)(2,1)S(1)} %get-tuple-element.141), channel_id=1, source_target_pairs={{0,1},{1,2},{2,3},{3,4},{4,5},{5,6},{6,7},{7,8},{8,9},{9,10},{10,1... | collective-permute-start | bytes 228104 | tf_op jit(solution)/shard_map/ppermute | solution.py:525
  212.6 9.6 %collective-permute-start.1 = (bf16[3,12672]{1,0:T(4,128)(2,1)S(1)}, bf16[3,12672]{1,0:T(4,128)(2,1)S(1)}, u32[]{:S(2)}, u32[]{:S(2)}) collective-permute-start(bf16[3,12672]{1,0:T(4,128)(2,1)S(1)} %get-tuple-element.142), channel_id=1, source_target_pairs={{1,0},{2,1},{3,2},{4,3},{5,4},{6,5},{7,6},{8,7},{9,8},{10,9},{11,1... | collective-permute-start | bytes 228104 | tf_op jit(solution)/shard_map/ppermute | solution.py:526

commit v7 on v6

--- a/solution.py
+++ b/solution.py
@@ -32,7 +32,7 @@
     blank.start()
 
     steps = a_ref.shape[0] // step_lanes
-    cuts = ((0, 4), (4, steps + 1))
+    cuts = ((0, 2), (2, steps + 1))
 
     def gathered(rows):
         return lax.dot_general(
@@ -320,7 +320,7 @@
             return tuple(accs)
 
         zero = jnp.zeros((half, LANES), f32)
-        return lax.fori_loop(0, tile // 8, body, (zero,) * modes)
+        return lax.fori_loop(0, tile // 8, body, (zero,) * modes, unroll=2)
 
     def each_part(fn):
         def body(q, carry):

time: 263 us -> 262 us (level)
  no operation moved by 1% of the time
where the time goes in v7:
time: 262 us
  Pallas kernels  221 us (84%)
  matrix products  10.6 us (4%)
  local copies, waits for them, and re-layouts  10.2 us (4%)
  waiting for transfers between devices  7.35 us (3%)
  starting transfers between devices  7.34 us (3%)
  other arithmetic  4.52 us (2%)
    pallas_call x1, Pallas kernels, exchange(): pl.pallas_call(functools.partial(exchange_kernel, members, slots, spill,...  176 us
    pallas_call x1, Pallas kernels, setup(): pl.pallas_call(setup_kernel, out_shape=(jax.ShapeDtypeStruct((3, modes, t...  35.1 us
    pallas_call x1, Pallas kernels, share_counts(): pl.pallas_call(functools.partial(counts_kernel, groups, members), out_sha...  9.25 us
    transpose x1, local copies, waits for them, and re-layouts, per_device(): a_rows = a_band.transpose(1, 3, 2, 0).reshape(size, rows)  9 us
    ppermute x1, waiting for transfers between devices, per_device(): from_right = lax.ppermute(rim[:HALO], axes, down)  7.34 us
    dot_general x1, matrix products, per_device(): jnp.dot(rim_pick, recv, preferred_element_type=jnp.float32).astype(bf16)  5.51 us
    ppermute x1, starting transfers between devices, per_device(): from_left = lax.ppermute(rim[HALO:2 * HALO], axes, up)  5.24 us
  transfers between devices with their start and end apart: 2, of which 1 were waited for; matrix products, arithmetic and copies ran while one was open for 0% of the time, Pallas kernels for 0%

profile of v7, /device:TPU:27, one launch (start us, length us, event | category | flops | bytes accessed | tf_op | source)
XLA Modules:
  0.0 262.1 jit_solution(17756502073550608500)
XLA Ops:
  0.6 0.0 copy-start.2
  0.6 0.0 copy-start.1
  0.7 0.9 convert_reduce_fusion
  1.5 0.5 pad_bitcast_fusion.own_ref
  2.0 9.2 %share_counts.1 = s32[32,1,128]{2,1,0:T(1,128)} custom-call(s32[1,128]{1,0:T(1,128)} %pad_bitcast_fusion.own_ref), custom_call_target="tpu_custom_call" | custom-call | tf_op jit(solution)/shard_map/share_counts/pallas_call | solution.py:268
  11.3 1.4 fusion.16
  12.7 0.3 dynamic-slice_reduce_fusion
  13.0 0.1 select_reduce_fusion.3
  13.2 0.1 add_select_fusion
  13.2 0.1 add_select_fusion.2
  13.3 0.9 fusion.4
  14.2 0.7 iota_compare_fusion.6
  14.9 0.1 select_reduce_fusion.2
  15.1 0.1 add_select_fusion.1
  15.1 0.1 select_n.96
  15.2 0.1 select_n.98
  15.3 0.1 select_n.93
  15.4 9.0 %copy.6 = bf16[3,64,64,192]{3,2,1,0:T(8,128)(2,1)} copy(bf16[3,64,64,192]{3,1,2,0:T(8,128)(2,1)} %bitcast.13) | data formatting | bytes 9437184 | tf_op jit(solution)/shard_map/transpose | solution.py:463
  24.4 0.6 reduce_max.9
  25.7 0.0 copy-done.2
  25.7 0.0 copy-done.1
  25.7 176.5 %conditional.1 = (bf16[400,12672]{1,0:T(8,128)(2,1)}) conditional(s32[]{:T(128)} %convert_element_type.28, (s32[192]{0:T(256)S(1)}, s32[192]{0:T(256)S(1)}, bf16[12288,192]{1,0:T(8,128)(2,1)}, bf16[384,192]{1,0:T(8,128)(2,1)S(1)}) %tuple.50, (s32[192]{0:T(256)S(1)}, s32[192]{0:T(256)S(1)}, s32[8]{0:T(128)S(1)}, pred[8,8]{1,0:T(8,128)(4,1)S(1)}, ...), branch_computations={%region_4.5_spmd, %region_5.8_spmd} | conditional | flops 147840 | bytes 150536 | solution.py:512
  25.8 0.1 select_reduce_fusion.1
  25.9 0.1 select_reduce_fusion
  26.0 176.2 %exchange_spill.2 = bf16[400,12672]{1,0:T(8,128)(2,1)} custom-call(bf16[272,192]{1,0:T(8,128)(2,1)S(1)} %fusion.1.pick_ref, bf16[12288,192]{1,0:T(8,128)(2,1)} %get-tuple-element.129.a_ref, bf16[384,192]{1,0:T(8,128)(2,1)S(1)} %get-tuple-element.130.p_ref), custom_call_target="tpu_custom_call" | custom-call | tf_op jit(solution)/shard_map/cond/branch_1_fun/exchange_spill/pallas_call | solution.py:206
  202.3 0.0 copy-start
  202.3 5.5 %convolution_convert_fusion.1 = bf16[16,12672]{1,0:T(8,128)(2,1)S(1)} fusion(bf16[400,12672]{1,0:T(8,128)(2,1)} %get-tuple-element.146, s32[400]{0:T(512)S(1)} %concatenate.13, s32[16]{0:T(128)S(1)} %compare_select_fusion.2), kind=kOutput, calls=%fused_computation.11 | convolution fusion | flops 162410752 | bytes 10544768 | tf_op jit(solution)/shard_map/dot_general | solution.py:521
  207.8 0.1 fusion.15
  207.9 5.2 %collective-permute-start = (bf16[3,12672]{1,0:T(4,128)(2,1)S(1)}, bf16[3,12672]{1,0:T(4,128)(2,1)S(1)}, u32[]{:S(2)}, u32[]{:S(2)}) collective-permute-start(bf16[3,12672]{1,0:T(4,128)(2,1)S(1)} %get-tuple-element.141), channel_id=1, source_target_pairs={{0,1},{1,2},{2,3},{3,4},{4,5},{5,6},{6,7},{7,8},{8,9},{9,10},{10,1... | collective-permute-start | bytes 228104 | tf_op jit(solution)/shard_map/ppermute | solution.py:525
  213.1 2.1 collective-permute-start.1
  215.3 0.1 pad.10.clone
  215.3 0.0 collective-permute-done
  215.4 7.3 %collective-permute-done.1 = bf16[3,12672]{1,0:T(4,128)(2,1)S(1)} collective-permute-done((bf16[3,12672]{1,0:T(4,128)(2,1)S(1)}, bf16[3,12672]{1,0:T(4,128)(2,1)S(1)}, u32[]{:S(2)}, u32[]{:S(2)}) %collective-permute-start.1) | collective-permute-done | bytes 76064 | tf_op jit(solution)/shard_map/ppermute | solution.py:526
  222.7 0.0 copy-done
  222.7 0.2 maximum_dynamic-update-slice_fusion
  222.9 4.1 %convolution_convert_fusion.ext_ref = bf16[12672,256]{1,0:T(8,128)(2,1)S(1)} fusion(bf16[400,12672]{1,0:T(8,128)(2,1)S(1)} %maximum_dynamic-update-slice_fusion, s32[400]{0:T(512)S(1)} %pad_add_fusion), kind=kOutput, calls=%fused_computation.10 | convolution fusion | flops 2598572032 | bytes 16627264 | tf_op jit(solution)/shard_map/dot_general | solution.py:534
  227.0 35.1 %coarse_setup.1 = (bf16[3,6,64,192]{3,2,1,0:T(8,128)(2,1)}, f32[192,252]{1,0:T(8,128)}) custom-call(bf16[12672,256]{1,0:T(8,128)(2,1)S(1)} %convolution_convert_fusion.ext_ref), custom_call_target="tpu_custom_call" | custom-call | tf_op jit(solution)/shard_map/coarse_setup/pallas_call | solution.py:414
  (16 shorter events, 0.1 us)
Async XLA Ops:
  0.6 25.1 %copy-start.2 = (s32[192]{0:T(256)S(1)}, s32[192]{0:T(256)}, u32[]{:S(2)}) copy-start(s32[192]{0:T(256)} %param.7) | copy-start | bytes 2308
  0.6 25.1 %copy-start.1 = (bf16[192,6,64]{0,2,1:T(8,128)(2,1)S(1)}, bf16[192,6,64]{0,2,1:T(8,128)(2,1)}, u32[]{:S(2)}) copy-start(bf16[192,6,64]{0,2,1:T(8,128)(2,1)} %param.6) | copy-start | bytes 442372
  202.3 20.4 %copy-start = (bf16[400,12672]{1,0:T(8,128)(2,1)S(1)}, bf16[400,12672]{1,0:T(8,128)(2,1)}, u32[]{:S(2)}) copy-start(bf16[400,12672]{1,0:T(8,128)(2,1)} %get-tuple-element.146) | copy-start | bytes 30412804
  207.9 7.5 %collective-permute-start = (bf16[3,12672]{1,0:T(4,128)(2,1)S(1)}, bf16[3,12672]{1,0:T(4,128)(2,1)S(1)}, u32[]{:S(2)}, u32[]{:S(2)}) collective-permute-start(bf16[3,12672]{1,0:T(4,128)(2,1)S(1)} %get-tuple-element.141), channel_id=1, source_target_pairs={{0,1},{1,2},{2,3},{3,4},{4,5},{5,6},{6,7},{7,8},{8,9},{9,10},{10,1... | collective-permute-start | bytes 228104 | tf_op jit(solution)/shard_map/ppermute | solution.py:525
  213.1 9.6 %collective-permute-start.1 = (bf16[3,12672]{1,0:T(4,128)(2,1)S(1)}, bf16[3,12672]{1,0:T(4,128)(2,1)S(1)}, u32[]{:S(2)}, u32[]{:S(2)}) collective-permute-start(bf16[3,12672]{1,0:T(4,128)(2,1)S(1)} %get-tuple-element.142), channel_id=1, source_target_pairs={{1,0},{2,1},{3,2},{4,3},{5,4},{6,5},{7,6},{8,7},{9,8},{10,9},{11,1... | collective-permute-start | bytes 228104 | tf_op jit(solution)/shard_map/ppermute | solution.py:526
